TPU v7x, 32 devices: a whole 2x2x4 slice. The times are simulated.
32 devices in a mesh: img: 2 (over y), dp: 16 (over z, x, core).
Axes of the slice: x: 2, y: 2, z: 4, core: 2. Of those that a mesh axis runs over, the one named last changes fastest.
Arguments:
- inputs: float32 [16, 768, 1152], P('dp', 'img'), may hold values from -16 to 16
- flat_params: bfloat16 [15253504], P(('img', 'dp')), may hold values from -2.5 to 2.5
- bias_table: bfloat16 [2816, 16], P(('img', 'dp')), may hold values from -1 to 252
- bucket_index: int32 [768, 768], replicated, may hold values from 0 to 2815, as said below
- valid_mask: int32 [16, 768], P('dp'), may hold values 0 or 1
- cotangent: float32 [16, 768, 1152], P('dp', 'img'), may hold values from -6 to 6
Outputs:
- layer_out: float32 [16, 768, 1152], P('dp', 'img')
- grad_inputs: float32 [16, 768, 1152], P('dp', 'img')
- grad_params: float32 [15253504], P(('img', 'dp'))
- grad_vectors: float32 [16384], P(('img', 'dp'))
- grad_table: float32 [2816, 16], P(('img', 'dp'))
Inputs may be any that keep to these rules, and one draw needn't show every extreme that they name: `bucket_index`: entry (i, j) is the bucket (r + 26) * 53 + c + 26 of the row and column offset (r, c) between the grid positions of the patches in token slots i and j on a 27 x 27 grid; every patch stands in one slot; pairs with an empty slot take bucket 2816 - 1.
All inputs are finite; a program needn't handle non-finite values. No bound on the sum of `valid_mask` on one device may be relied on, other than what follows from the above.
Results may differ from a plain program's by a relative error of at most 0.0085.
Values may be sent and summed in bfloat16 or wider, within the bound.
No kernel may reach another device: no remote copies, remote signals or barrier semaphores. Data moves between devices by JAX's collectives and lax.ppermute only.
A program may use at most 704 MiB of HBM per device.

v0:
```python
import math

import jax
import jax.numpy as jnp
from jax import lax
from jax.sharding import PartitionSpec as P

D = 1152
FF = 4304
PARAMS_PAD = 15253504
VEC_PAD = 16384


EPS = 1e-06
PENALTY = 30000.0
GELU_C = math.sqrt(2.0 / math.pi)
GELU_K = 0.044715


def contract_rows(left_side, right_side):
    return lax.dot_general(
        left_side, right_side, (((0,), (0,)), ((), ())), preferred_element_type=jnp.float32
    )


def times_transposed(left_side, right_side):
    return lax.dot_general(
        left_side, right_side, (((1,), (1,)), ((), ())), preferred_element_type=jnp.float32
    )


def segment_lengths(model_width, hidden_width):
    return (
        [
            3 * model_width * model_width,
            model_width * model_width,
            model_width * hidden_width,
            hidden_width * model_width,
        ]
        + [model_width] * 8
        + [hidden_width]
    )


def unpack(flat_full, model_width, hidden_width):
    segments = []
    cursor = 0
    for length in segment_lengths(model_width, hidden_width):
        segments.append(flat_full[cursor : cursor + length])
        cursor = cursor + length
    w_qkv = segments[0].reshape(model_width, 3 * model_width)
    w_out = segments[1].reshape(model_width, model_width)
    w_up = segments[2].reshape(model_width, hidden_width)
    w_down = segments[3].reshape(hidden_width, model_width)
    vectors = [segment.astype(jnp.float32) for segment in segments[4:]]
    return (w_qkv, w_out, w_up, w_down, vectors)


def pack(gradients, padded_total):
    flat_grad = jnp.concatenate([grad_piece.reshape(-1) for grad_piece in gradients])
    return jnp.concatenate(
        [flat_grad, jnp.zeros((padded_total - flat_grad.shape[0],), jnp.float32)]
    )


def layer_norm(stream, gain, shift):
    centered = stream - jnp.mean(stream, axis=-1, keepdims=True)
    inv_std = lax.rsqrt(jnp.mean(centered * centered, axis=-1, keepdims=True) + EPS)
    normed = centered * inv_std
    return (normed * gain + shift, normed, inv_std)


def norm_back(grad_out, normed, inv_std, gain):
    grad_normed = grad_out * gain
    grad_in = inv_std * (
        grad_normed
        - jnp.mean(grad_normed, axis=-1, keepdims=True)
        - normed * jnp.mean(grad_normed * normed, axis=-1, keepdims=True)
    )
    return (grad_in, jnp.sum(grad_out * normed, axis=0), jnp.sum(grad_out, axis=0))


def gelu_parts(pre_act):
    tanh_val = jnp.tanh(GELU_C * (pre_act + GELU_K * pre_act**3))
    activated = 0.5 * pre_act * (1.0 + tanh_val)
    derivative = 0.5 * (1.0 + tanh_val) + 0.5 * pre_act * (1.0 - tanh_val * tanh_val) * GELU_C * (
        1.0 + 3.0 * GELU_K * pre_act * pre_act
    )
    return (activated, derivative)


def split_heads(rows_in, head_count):
    return rows_in.reshape(rows_in.shape[0], head_count, -1)


def score_block(query_heads, key_heads, bias_terms, valid_keys):
    head_dim = query_heads.shape[-1]
    logits = jnp.einsum("qhd,khd->hqk", query_heads, key_heads, preferred_element_type=jnp.float32)
    penalty_row = PENALTY * (1.0 - valid_keys.astype(jnp.float32))
    return logits * head_dim ** (-0.5) + bias_terms - penalty_row[None, None, :]


def fetch(flat_params, bias_table):
    return (
        lax.all_gather(flat_params, ("img", "dp"), axis=0, tiled=True),
        lax.all_gather(bias_table, ("img", "dp"), axis=0, tiled=True),
    )


def settle(flat_grad, vector_grad, table_grad):
    return (
        lax.psum_scatter(flat_grad, ("img", "dp"), scatter_dimension=0, tiled=True),
        lax.psum_scatter(vector_grad, ("img", "dp"), scatter_dimension=0, tiled=True),
        lax.psum_scatter(table_grad, ("img", "dp"), scatter_dimension=0, tiled=True),
    )


def local(inputs, flat_params, bias_table, bucket_index, valid_mask, cotangent):
    images, local_rows, model_width = inputs.shape
    head_count = bias_table.shape[1]
    row_count = images * local_rows
    flat_full, table_full = fetch(flat_params, bias_table)
    bucket_rows = table_full.shape[0]
    w_qkv, w_out, w_up, w_down, vectors = unpack(flat_full, D, FF)
    (
        norm1_gain,
        norm1_shift,
        bias_query,
        bias_value,
        bias_out,
        norm2_gain,
        norm2_shift,
        bias_down,
        bias_up,
    ) = vectors
    first_row = lax.axis_index("img") * local_rows
    local_buckets = lax.dynamic_slice_in_dim(bucket_index, first_row, local_rows, 0)
    table_heads = table_full.astype(jnp.float32).T
    bias_terms = jnp.take(table_heads, local_buckets, axis=1)
    flat_local = local_buckets.reshape(-1)

    def head_segments(head_scores):
        return jax.ops.segment_sum(head_scores, flat_local, num_segments=bucket_rows)

    stream = inputs.reshape(row_count, model_width)
    attn_full, normed1, inv_std1 = layer_norm(stream, norm1_gain, norm1_shift)
    attn_in = attn_full.astype(jnp.bfloat16)
    projected = jnp.dot(attn_in, w_qkv, preferred_element_type=jnp.float32)
    query_rows = (projected[:, :model_width] + bias_query).astype(jnp.bfloat16)
    key_rows = projected[:, model_width : 2 * model_width].astype(jnp.bfloat16)
    value_rows = (projected[:, 2 * model_width :] + bias_value).astype(jnp.bfloat16)
    pair_local = jnp.concatenate([key_rows, value_rows], axis=-1).reshape(
        images, local_rows, 2 * model_width
    )
    pair_full = lax.all_gather(pair_local, "img", axis=1, tiled=True)
    query_stack = query_rows.reshape(images, local_rows, model_width)

    def forward_image(image_args):
        query_block, pair_block, valid_keys = image_args
        query_heads = split_heads(query_block, head_count)
        key_heads = split_heads(pair_block[:, :model_width], head_count)
        value_heads = split_heads(pair_block[:, model_width:], head_count)
        scores = score_block(query_heads, key_heads, bias_terms, valid_keys)
        row_max = jnp.max(scores, axis=-1, keepdims=True)
        exp_scores = jnp.exp(scores - row_max)
        row_total = jnp.sum(exp_scores, axis=-1, keepdims=True)
        attn_probs = (exp_scores / row_total).astype(jnp.bfloat16)
        attn_heads = jnp.einsum(
            "hqk,khd->qhd", attn_probs, value_heads, preferred_element_type=jnp.float32
        )
        return (
            attn_heads.reshape(local_rows, model_width).astype(jnp.bfloat16),
            row_max + jnp.log(row_total),
        )

    attn_stack, log_norm = lax.map(forward_image, (query_stack, pair_full, valid_mask))
    attn_mixed = attn_stack.reshape(row_count, model_width)
    resid = stream + jnp.dot(attn_mixed, w_out, preferred_element_type=jnp.float32) + bias_out
    mlp_full, normed2, inv_std2 = layer_norm(resid, norm2_gain, norm2_shift)
    mlp_in = mlp_full.astype(jnp.bfloat16)
    pre_act = jnp.dot(mlp_in, w_up, preferred_element_type=jnp.float32) + bias_up
    activated, derivative = gelu_parts(pre_act)
    hidden_act = activated.astype(jnp.bfloat16)
    output = resid + jnp.dot(hidden_act, w_down, preferred_element_type=jnp.float32) + bias_down
    grad_out = cotangent.reshape(row_count, model_width)
    grad_out_b = grad_out.astype(jnp.bfloat16)
    g_w_down = contract_rows(hidden_act, grad_out_b)
    g_b_down = jnp.sum(grad_out, axis=0)
    grad_pre = times_transposed(grad_out_b, w_down) * derivative
    grad_pre_b = grad_pre.astype(jnp.bfloat16)
    g_w_up = contract_rows(mlp_in, grad_pre_b)
    g_b_up = jnp.sum(grad_pre, axis=0)
    resid_part, g_n2_gain, g_n2_shift = norm_back(
        times_transposed(grad_pre_b, w_up), normed2, inv_std2, norm2_gain
    )
    grad_resid = grad_out + resid_part
    grad_resid_b = grad_resid.astype(jnp.bfloat16)
    g_w_out = contract_rows(attn_mixed, grad_resid_b)
    g_b_out = jnp.sum(grad_resid, axis=0)
    grad_mixed = times_transposed(grad_resid_b, w_out).astype(jnp.bfloat16)

    def backward_image(table_sum, image_args):
        query_block, pair_block, valid_keys, norm_block, grad_block = image_args
        query_heads = split_heads(query_block, head_count)
        key_heads = split_heads(pair_block[:, :model_width], head_count)
        value_heads = split_heads(pair_block[:, model_width:], head_count)
        scores = score_block(query_heads, key_heads, bias_terms, valid_keys)
        back_probs = jnp.exp(scores - norm_block)
        grad_heads = split_heads(grad_block, head_count)
        grad_probs = jnp.einsum(
            "qhd,khd->hqk", grad_heads, value_heads, preferred_element_type=jnp.float32
        )
        row_dot = jnp.sum(back_probs * grad_probs, axis=-1, keepdims=True)
        grad_scores = back_probs * (grad_probs - row_dot)
        table_part = jax.vmap(head_segments)(grad_scores.reshape(head_count, -1)).T
        grad_scores_b = grad_scores.astype(jnp.bfloat16)
        probs_b = back_probs.astype(jnp.bfloat16)
        scale_factor = query_heads.shape[-1] ** (-0.5)
        grad_query = scale_factor * jnp.einsum(
            "hqk,khd->qhd", grad_scores_b, key_heads, preferred_element_type=jnp.float32
        )
        grad_key = scale_factor * jnp.einsum(
            "hqk,qhd->khd", grad_scores_b, query_heads, preferred_element_type=jnp.float32
        )
        grad_value = jnp.einsum(
            "hqk,qhd->khd", probs_b, grad_heads, preferred_element_type=jnp.float32
        )
        key_count = pair_block.shape[0]
        grad_pair = jnp.concatenate(
            [grad_key.reshape(key_count, model_width), grad_value.reshape(key_count, model_width)],
            axis=-1,
        )
        return (table_sum + table_part, (grad_query.reshape(local_rows, model_width), grad_pair))

    start_sum = jnp.zeros((bucket_rows, head_count), jnp.float32)
    table_grad, (grad_query, grad_pair) = lax.scan(
        backward_image,
        start_sum,
        (
            query_stack,
            pair_full,
            valid_mask,
            log_norm,
            grad_mixed.reshape(images, local_rows, model_width),
        ),
    )
    pair_grads = lax.psum_scatter(grad_pair, "img", scatter_dimension=1, tiled=True)
    grad_query = grad_query.reshape(row_count, model_width)
    grad_key = pair_grads[:, :, :model_width].reshape(row_count, model_width)
    grad_value = pair_grads[:, :, model_width:].reshape(row_count, model_width)
    grad_proj_b = jnp.concatenate([grad_query, grad_key, grad_value], axis=-1).astype(jnp.bfloat16)
    g_w_qkv = contract_rows(attn_in, grad_proj_b)
    g_b_query = jnp.sum(grad_query, axis=0)
    g_b_value = jnp.sum(grad_value, axis=0)
    input_part, g_n1_gain, g_n1_shift = norm_back(
        times_transposed(grad_proj_b, w_qkv), normed1, inv_std1, norm1_gain
    )
    grad_in = grad_resid + input_part
    flat_grad = pack([g_w_qkv, g_w_out, g_w_up, g_w_down], PARAMS_PAD)
    vector_grad = pack(
        [
            g_n1_gain,
            g_n1_shift,
            g_b_query,
            g_b_value,
            g_b_out,
            g_n2_gain,
            g_n2_shift,
            g_b_down,
            g_b_up,
        ],
        VEC_PAD,
    )
    owned_flat, owned_vector, owned_table = settle(flat_grad, vector_grad, table_grad)
    return (
        output.reshape(images, local_rows, model_width),
        grad_in.reshape(images, local_rows, model_width),
        owned_flat,
        owned_vector,
        owned_table,
    )


def solution(mesh):
    placed = (
        P("dp", "img", None),
        P(("img", "dp")),
        P(("img", "dp"), None),
        P(),
        P("dp", None),
        P("dp", "img", None),
    )
    return jax.shard_map(
        local,
        mesh=mesh,
        in_specs=placed,
        out_specs=(
            P("dp", "img", None),
            P("dp", "img", None),
            P(("img", "dp")),
            P(("img", "dp")),
            P(("img", "dp"), None),
        ),
        check_vma=False,
    )
```

profile of v0, /device:TPU:0, one launch (start us, length us, event | category | flops | bytes accessed | tf_op | source)
XLA Modules:
  0.0 4379.7 jit_solution(6522096479467159521)
XLA Ops:
  17.9 44.8 %all-gather.2 = bf16[32,88,16]{1,2,0:T(8,128)(2,1)S(1)} all-gather(bf16[1,88,16]{1,2,0:T(8,128)(2,1)S(1)} %bitcast.118), channel_id=1, replica_groups=mesh['img'=2,'dp'=16] {'img','dp'}, dimensions={0}, use_global_device_ids=true | all-gather | bytes 92928 | tf_op jit(solution)/shard_map/all_gather | solution.py:106
  69.1 974.0 %gather_fusion = f32[294912,16]{1,0:T(8,128)} fusion(f32[16,2816]{0,1:T(8,128)S(1)} %bitcast.98, s32[294912]{0:T(1024)S(1)} %broadcast_clamp_fusion), kind=kCustom, calls=%fused_computation | custom fusion | bytes 38928384 | tf_op jit(solution)/shard_map/jit(_take)/gather | solution.py:139
  1043.1 82.4 %copy.42 = f32[384,768,16]{1,0,2:T(8,128)} copy(f32[384,768,16]{2,1,0:T(8,128)} %bitcast.8) | data formatting | bytes 37748736 | tf_op jit(solution)/shard_map/jit(_take)/gather | solution.py:139
  1126.7 177.0 %reduce.4 = bf16[32,476672]{1,0:T(8,128)(2,1)} reduce(bf16[32,1,476672]{2,1,0:T(2,128)(2,1)} %all-gather.8.cloned.1.call-done, bf16[]{:T(256)} %constant.123), dimensions={1}, to_apply=%all-gather.1.reduce_sub_computation | reduce | bytes 61014016 | tf_op jit(solution)/shard_map/all_gather | solution.py:105
  1303.7 70.6 %reshape.266 = bf16[15253504]{0:T(1024)(128)(2,1)} reshape(bf16[32,476672]{1,0:T(8,128)(2,1)} %reduce.4) | data formatting | bytes 61014016
  1382.7 15.2 reshape.222
  1406.2 15.8 fusion.59
  1427.8 20.1 reshape.228
  1448.8 19.6 reshape.229
  1480.6 12.9 fusion.61
  1525.3 14.3 fusion.63
  1556.3 11.6 fusion.3
  1567.9 17.3 multiply_reduce_fusion
  1585.3 15.6 subtract_multiply_fusion
  1617.4 71.4 %copy.43 = f32[16,384,768]{0,2,1:T(8,128)} copy(f32[16,384,768]{2,1,0:T(8,128)} %subtract_multiply_fusion) | data formatting | bytes 37748736 | tf_op jit(solution)/shard_map/while/body/eval_jaxpr/reshape | solution.py:215
  1700.6 15.8 fusion.38
  1716.4 20.9 reshape.242
  1737.4 11.6 fusion.27
  1749.0 25.7 reshape.241
  1787.3 1582.6 %scatter_custom_fusion = f32[16,2816]{0,1:T(8,128)} fusion(s32[294912]{0:T(1024)} %reshape.254, f32[294912,16]{1,0:T(8,128)} %bitcast.28, f32[]{:T(128)} %constant.59.clone.1), kind=kCustom, calls=%fused_computation.91 | custom fusion | flops 4718592 | bytes 180736 | tf_op jit(solution)/shard_map/while/body/eval_jaxpr/vmap()/scatter-add | solution.py:143
  3392.9 16.7 reshape.239
  3425.4 17.4 constant_dynamic-update-slice_fusion.1
  3466.5 38.8 reduce-scatter.8.cloned.1.call-done
  3511.9 856.2 %all-reduce.6.cloned.1.call-done = (f32[15253504]{0:T(1024)}, f32[16384]{0:T(1024)}) async-done(((f32[15253504]{0:T(1024)}, f32[16384]{0:T(1024)}), (f32[15253504]{0:T(1024)}, f32[16384]{0:T(1024)})) %all-reduce.6.cloned.1.call-update) | async-done | bytes 61079568
  (183 shorter events, 216.7 us)
Async XLA Ops:
  7.2 1119.5 %all-gather.8.cloned.1.call-start = ((), (), s32[]{:S(2)}) async-start(), calls=%async_computation.4 | async-start | bytes 62920704 | tf_op jit(solution)/shard_map/all_gather | solution.py:105
  17.9 1451.8 %all-gather.6.cloned.1.call-start = ((), (), s32[]{:S(2)}) async-start(), calls=%async_computation.3 | async-start | bytes 5308416 | tf_op jit(solution)/shard_map/all_gather | solution.py:155
  1043.1 82.4 %copy-start.1 = (f32[1,384,1152]{2,1,0:T(8,128)S(1)}, f32[1,384,1152]{2,1,0:T(8,128)}, u32[]{:S(2)}) copy-start(f32[1,384,1152]{2,1,0:T(8,128)} %param.6) | copy-start | bytes 5308420
  1043.1 82.6 %copy-start.41 = (s32[1,768]{1,0:T(1,128)S(1)}, s32[1,768]{1,0:T(1,128)}, u32[]{:S(2)}) copy-start(s32[1,768]{1,0:T(1,128)} %param.10) | copy-start | bytes 9220
  1126.3 271.6 %copy-start.27 = (f32[384]{0:T(512)}, f32[384]{0:T(512)S(1)}, u32[]{:S(2)}) copy-start(f32[384]{0:T(512)S(1)} %broadcast_multiply_fusion.5) | copy-start | bytes 4612
  1126.6 271.3 %copy-start.32 = (f32[384]{0:T(512)}, f32[384]{0:T(512)S(1)}, u32[]{:S(2)}) copy-start(f32[384]{0:T(512)S(1)} %add_rsqrt_fusion.1) | copy-start | bytes 4612
  1375.7 22.2 copy-start.22
  1375.7 22.2 copy-start.25
  1375.7 138.3 %copy-start.29 = (f32[1152]{0:T(1024)}, f32[1152]{0:T(1024)S(1)}, u32[]{:S(2)}) copy-start(f32[1152]{0:T(1024)S(1)} %get-tuple-element.90) | copy-start | bytes 13828
  1406.1 1963.8 %reduce-scatter.6.cloned.1.call-start = ((), (), s32[]{:S(2)}) async-start(), calls=%async_computation.2 | async-start | bytes 10616832 | tf_op jit(solution)/shard_map/reduce_scatter | solution.py:247
  1448.8 31.8 copy-start.13
  1480.6 23.4 copy-start.15
  1513.7 36.7 copy-start.34
  1514.0 36.4 copy-start.36
  1551.6 137.2 %copy-start.6 = (f32[384,1152]{1,0:T(8,128)}, f32[384,1152]{1,0:T(8,128)S(1)}, u32[]{:S(2)}) copy-start(f32[384,1152]{1,0:T(8,128)S(1)} %get-tuple-element.85) | copy-start | bytes 5308420
  1556.2 29.0 slice-start
  1556.3 29.0 slice-start.1
  1612.6 1892.8 %reduce-scatter.8.cloned.1.call-start = ((), (), s32[]{:S(2)}) async-start(), calls=%async_computation.5 | async-start | bytes 1486848
  1749.0 25.7 copy-start.5
  1785.7 1586.5 %copy-start.3 = (f32[1,384,1152]{2,1,0:T(8,128)S(1)}, f32[1,384,1152]{2,1,0:T(8,128)}, u32[]{:S(2)}) copy-start(f32[1,384,1152]{2,1,0:T(8,128)} %param.6) | copy-start | bytes 5308420
  1785.7 1586.6 %copy-start.23 = (f32[1152]{0:T(1024)S(1)}, f32[1152]{0:T(1024)}, u32[]{:S(2)}) copy-start(f32[1152]{0:T(1024)} %copy-done.22) | copy-start | bytes 13828
  1785.7 1586.6 %copy-start.28 = (f32[384]{0:T(512)S(1)}, f32[384]{0:T(512)}, u32[]{:S(2)}) copy-start(f32[384]{0:T(512)} %copy-done.27) | copy-start | bytes 4612
  1785.7 1586.6 %copy-start.33 = (f32[384]{0:T(512)S(1)}, f32[384]{0:T(512)}, u32[]{:S(2)}) copy-start(f32[384]{0:T(512)} %copy-done.32) | copy-start | bytes 4612
  3369.9 998.2 %all-reduce.6.cloned.1.call-start = ((), (), s32[]{:S(2)}) async-start(), calls=%async_computation.6 | async-start | bytes 122159104
  (34 other events, 398.8 us)
Sparse Core Ops, SparseCore 0:
  18.0 330.0 all-gather.7
  1406.3 45.5 all-gather.5
  1612.7 81.7 reduce-scatter.5
  3370.0 135.2 reduce-scatter.7
  3511.6 856.4 all-reduce.5
where the time goes:
time: 4390 us; the launch traced here: 4380 us
  other arithmetic  1810 us (41%)
  local copies, waits for them, and re-layouts  1440 us (33%)
  waiting for transfers between devices  895 us (20%)
  matrix products  178 us (4%)
  blocking collectives  44.8 us (1%)
    scatter-add x1, other arithmetic, head_segments(): jax.ops.segment_sum(head_scores, flat_local, num_segments=bucket_rows)  1580 us
    gather x2, local copies, waits for them, and re-layouts, local(): bias_terms = jnp.take(table_heads, local_buckets, axis=1)  1060 us
    unnamed x7, waiting for transfers between devices  895 us
    all_gather x1, other arithmetic, fetch(): lax.all_gather(flat_params, ('img', 'dp'), axis=0, tiled=True)  177 us
    unnamed x113, local copies, waits for them, and re-layouts  132 us
  transfers between devices with their start and end apart: 5, of which 2 were waited for; matrix products, arithmetic and copies ran while one was open for 68% of the time, Pallas kernels for 0%

commit v1 on v0

v1 whole, which is shorter than its diff:
```python
import math

import jax
import jax.numpy as jnp
from jax import lax
from jax.experimental import pallas as pl
from jax.experimental.pallas import tpu as pltpu
from jax.sharding import PartitionSpec as P

D = 1152
FF = 4304
FFP = 4352
H = 16
HL = 8
DH = 72
SEQ = 768
GRID = 27
SPAN = 53
NB = 2816
PARAMS_PAD = 15253504
VEC_PAD = 16384
EPS = 1e-06
PENALTY = 30000.0
ABSENT = -1e30
GELU_C = math.sqrt(2.0 / math.pi)
GELU_K = 0.044715
SCALE = DH ** (-0.5)

LP = 896
EW = 1792
BF = jnp.bfloat16
F32 = jnp.float32

Q_END = 3 * D * D
O_END = Q_END + D * D
U_END = O_END + D * FF
D_END = U_END + FF * D
VECTORS = 8 * D + FF


def dot(a, b, ca, cb):
    return lax.dot_general(a, b, (((ca,), (cb,)), ((), ())), preferred_element_type=F32)


def offset_of(key_row):
    lead = 26 - key_row
    return lead % 4, (lead // 4) * 128


def wide(column):
    return jnp.concatenate([column] * (LP // 128), axis=1)


def shift_bias(e_ref, e4):
    bias = e_ref[0]
    e4[0] = bias
    for m in range(1, 4):
        e4[m] = pltpu.roll(bias, EW - 32 * m, 1)


def attend_forward(q_ref, k_ref, v_ref, e_ref, pen_ref, out_ref, norm_ref, e4, s_scr, p_scr):
    shift_bias(e_ref, e4)
    q = q_ref[0, 0]
    k = k_ref[0, 0]
    top = jnp.full((32, LP), -jnp.inf, F32)
    for kb in range(7):
        s = dot(k[:, kb * 128 : (kb + 1) * 128], q, 0, 0)
        for sub in range(4):
            row = kb * 4 + sub
            lo = row * 32
            part = s[sub * 32 : sub * 32 + 32] * SCALE
            if row < GRID:
                m, base = offset_of(row)
                part = part + e4[m, :, base : base + LP]
            part = part + wide(pen_ref[lo : lo + 32])
            s_scr[lo : lo + 32] = part
            top = jnp.maximum(top, part)
    row_max = jnp.max(top, axis=0, keepdims=True)
    total = jnp.zeros((32, LP), F32)
    for row in range(28):
        lo = row * 32
        p = jnp.exp(s_scr[lo : lo + 32] - row_max)
        total = total + p
        p_scr[lo : lo + 32] = p.astype(BF)
    row_total = jnp.sum(total, axis=0, keepdims=True)
    mixed = dot(v_ref[0, 0], p_scr[...], 1, 0)
    out_ref[0] = (mixed / row_total).astype(BF)
    norm_ref[0] = row_max + jnp.log(row_total)


def attend_backward(
    q_ref, k_ref, v_ref, do_ref, e_ref, pen_ref, norm_ref,
    grad_ref, acc_ref, sums_ref,
    e4, p_scr, g_scr, pb_scr, gb_scr, acc,
):
    shift_bias(e_ref, e4)
    q = q_ref[0, 0]
    k = k_ref[0, 0]
    v = v_ref[0, 0]
    do = do_ref[0]
    log_norm = norm_ref[0]
    along = jnp.zeros((32, LP), F32)
    for kb in range(7):
        cols = slice(kb * 128, (kb + 1) * 128)
        s = dot(k[:, cols], q, 0, 0)
        g = dot(v[:, cols], do, 0, 0)
        for sub in range(4):
            row = kb * 4 + sub
            lo = row * 32
            part = s[sub * 32 : sub * 32 + 32] * SCALE
            if row < GRID:
                m, base = offset_of(row)
                part = part + e4[m, :, base : base + LP]
            part = part + wide(pen_ref[lo : lo + 32])
            p = jnp.exp(part - log_norm)
            g_part = g[sub * 32 : sub * 32 + 32]
            along = along + p * g_part
            p_scr[lo : lo + 32] = p
            g_scr[lo : lo + 32] = g_part
            pb_scr[lo : lo + 32] = p.astype(BF)
    row_dot = jnp.sum(along, axis=0, keepdims=True)
    acc[...] = jnp.zeros_like(acc)
    for row in range(28):
        lo = row * 32
        ds = p_scr[lo : lo + 32] * (g_scr[lo : lo + 32] - row_dot)
        if row < GRID:
            m, base = offset_of(row)
            acc[m, :, base : base + LP] += ds
        gb_scr[lo : lo + 32] = ds.astype(BF)
    total = acc[0]
    for m in range(1, 4):
        total = total + pltpu.roll(acc[m], 32 * m, 1)
    acc_ref[0] = total
    gb = gb_scr[...]
    dq = dot(k, gb, 1, 0) * SCALE
    dk = dot(q, gb, 1, 1) * SCALE
    dv = dot(do, pb_scr[...], 1, 1)
    grad_ref[0, 0] = dq.astype(BF)
    grad_ref[1, 0] = dk.astype(BF)
    grad_ref[2, 0] = dv.astype(BF)
    sums_ref[0, 0] = jnp.broadcast_to(jnp.sum(dq, axis=1, keepdims=True), (DH, 128))
    sums_ref[1, 0] = jnp.broadcast_to(jnp.sum(dv, axis=1, keepdims=True), (DH, 128))


def head_block(which):
    return pl.BlockSpec((1, 1, DH, LP), lambda h: (which, h, 0, 0))


def run_forward(qkv, bias, pen):
    return pl.pallas_call(
        attend_forward,
        grid=(HL,),
        in_specs=[
            head_block(0),
            head_block(1),
            head_block(2),
            pl.BlockSpec((1, 32, EW), lambda h: (h, 0, 0)),
            pl.BlockSpec((LP, 128), lambda h: (0, 0)),
        ],
        out_specs=[
            pl.BlockSpec((1, DH, LP), lambda h: (h, 0, 0)),
            pl.BlockSpec((1, 1, LP), lambda h: (h, 0, 0)),
        ],
        out_shape=[
            jax.ShapeDtypeStruct((HL, DH, LP), BF),
            jax.ShapeDtypeStruct((HL, 1, LP), F32),
        ],
        scratch_shapes=[
            pltpu.VMEM((4, 32, EW), F32),
            pltpu.VMEM((LP, LP), F32),
            pltpu.VMEM((LP, LP), BF),
        ],
        compiler_params=pltpu.CompilerParams(vmem_limit_bytes=48 * 2**20),
        cost_estimate=pl.CostEstimate(
            flops=HL * 4 * LP * LP * 128, bytes_accessed=8 * 2**20, transcendentals=HL * LP * LP
        ),
        name="attend_forward",
    )(qkv, qkv, qkv, bias, pen)


def run_backward(qkv, d_mixed, bias, pen, log_norm):
    return pl.pallas_call(
        attend_backward,
        grid=(HL,),
        in_specs=[
            head_block(0),
            head_block(1),
            head_block(2),
            pl.BlockSpec((1, DH, LP), lambda h: (h, 0, 0)),
            pl.BlockSpec((1, 32, EW), lambda h: (h, 0, 0)),
            pl.BlockSpec((LP, 128), lambda h: (0, 0)),
            pl.BlockSpec((1, 1, LP), lambda h: (h, 0, 0)),
        ],
        out_specs=[
            pl.BlockSpec((3, 1, DH, LP), lambda h: (0, h, 0, 0)),
            pl.BlockSpec((1, 32, EW), lambda h: (h, 0, 0)),
            pl.BlockSpec((2, 1, DH, 128), lambda h: (0, h, 0, 0)),
        ],
        out_shape=[
            jax.ShapeDtypeStruct((3, HL, DH, LP), BF),
            jax.ShapeDtypeStruct((HL, 32, EW), F32),
            jax.ShapeDtypeStruct((2, HL, DH, 128), F32),
        ],
        scratch_shapes=[
            pltpu.VMEM((4, 32, EW), F32),
            pltpu.VMEM((LP, LP), F32),
            pltpu.VMEM((LP, LP), F32),
            pltpu.VMEM((LP, LP), BF),
            pltpu.VMEM((LP, LP), BF),
            pltpu.VMEM((4, 32, EW), F32),
        ],
        compiler_params=pltpu.CompilerParams(vmem_limit_bytes=48 * 2**20),
        cost_estimate=pl.CostEstimate(
            flops=HL * 10 * LP * LP * 128, bytes_accessed=16 * 2**20, transcendentals=HL * LP * LP
        ),
        name="attend_backward",
    )(qkv, qkv, qkv, d_mixed, bias, pen, log_norm)


FB = 256


def mlp_body(
    x_ref, xt_ref, go_ref, up_ref, down_ref, bias_ref,
    out_ref, gx_ref, g_up_ref, g_down_ref, g_bias_ref,
):
    step = pl.program_id(0)

    @pl.when(step == 0)
    def _():
        out_ref[...] = jnp.zeros_like(out_ref)
        gx_ref[...] = jnp.zeros_like(gx_ref)

    go = go_ref[...]
    up = up_ref[...]
    down = down_ref[...]
    pre = dot(x_ref[...], up, 1, 0) + bias_ref[...]
    square = pre * pre
    t = jnp.tanh(GELU_C * (pre + GELU_K * (square * pre)))
    half = 0.5 * (1.0 + t)
    hidden = (pre * half).astype(BF)
    slope = half + 0.5 * pre * (1.0 - t * t) * (GELU_C * (1.0 + 3.0 * GELU_K * square))
    out_ref[...] += dot(hidden, down, 1, 0)
    g_down_ref[...] = dot(hidden, go, 0, 0).astype(BF)
    grad_pre = dot(go, down, 1, 1) * slope
    g_bias_ref[...] = jnp.sum(grad_pre, axis=0, keepdims=True)
    grad_pre_b = grad_pre.astype(BF)
    g_up_ref[...] = dot(xt_ref[...], grad_pre_b, 1, 0).astype(BF)
    gx_ref[...] += dot(grad_pre_b, up, 1, 1)


def run_mlp(x, grad_out, w_up, w_down, bias_up):
    rows = x.shape[0]
    whole = lambda shape: pl.BlockSpec(shape, lambda j: (0, 0))
    return pl.pallas_call(
        mlp_body,
        grid=(FFP // FB,),
        in_specs=[
            whole((rows, D)),
            whole((D, rows)),
            whole((rows, D)),
            pl.BlockSpec((D, FB), lambda j: (0, j)),
            pl.BlockSpec((FB, D), lambda j: (j, 0)),
            pl.BlockSpec((1, FB), lambda j: (0, j)),
        ],
        out_specs=[
            whole((rows, D)),
            whole((rows, D)),
            pl.BlockSpec((D, FB), lambda j: (0, j)),
            pl.BlockSpec((FB, D), lambda j: (j, 0)),
            pl.BlockSpec((1, FB), lambda j: (0, j)),
        ],
        out_shape=[
            jax.ShapeDtypeStruct((rows, D), F32),
            jax.ShapeDtypeStruct((rows, D), F32),
            jax.ShapeDtypeStruct((D, FFP), BF),
            jax.ShapeDtypeStruct((FFP, D), BF),
            jax.ShapeDtypeStruct((1, FFP), F32),
        ],
        compiler_params=pltpu.CompilerParams(vmem_limit_bytes=48 * 2**20),
        cost_estimate=pl.CostEstimate(
            flops=12 * rows * D * FFP, bytes_accessed=50 * 2**20, transcendentals=rows * FFP
        ),
        name="mlp_both_ways",
    )(x, x.T, grad_out, w_up, w_down, bias_up)


def layer_norm(stream, gain, shift):
    centered = stream - jnp.mean(stream, axis=-1, keepdims=True)
    inv_std = lax.rsqrt(jnp.mean(centered * centered, axis=-1, keepdims=True) + EPS)
    normed = centered * inv_std
    return (normed * gain + shift, normed, inv_std)


def norm_back(grad_out, normed, inv_std, gain):
    grad_normed = grad_out * gain
    grad_in = inv_std * (
        grad_normed
        - jnp.mean(grad_normed, axis=-1, keepdims=True)
        - normed * jnp.mean(grad_normed * normed, axis=-1, keepdims=True)
    )
    return (grad_in, jnp.sum(grad_out * normed, axis=0), jnp.sum(grad_out, axis=0))


def slot_places(bucket_index):
    real = bucket_index < SPAN * SPAN
    row = jnp.max(jnp.where(real, bucket_index // SPAN, -1), axis=1) - (GRID - 1)
    col = jnp.max(jnp.where(real, bucket_index % SPAN, -1), axis=1) - (GRID - 1)
    empty = row < 0
    earlier = jnp.arange(SEQ)[:, None] > jnp.arange(SEQ)[None, :]
    rank = jnp.sum(jnp.where(earlier & empty[None, :], 1, 0), axis=1)
    spare = (rank // 5) * 32 + GRID + rank % 5
    return jnp.where(empty, spare, row * 32 + col)


def column_classes():
    key_col = jnp.arange(1024)[:, None] // 32
    query_col = jnp.arange(1024)[:, None] % 32
    kind = jnp.where((key_col < GRID) & (query_col < GRID), query_col - key_col + GRID - 1, SPAN)
    return jnp.arange(SPAN + 1)[None, :] == kind


def spread_table(table_heads):
    heads = table_heads.shape[0]
    body = table_heads[:, : SPAN * SPAN].reshape(heads, SPAN, SPAN)
    last = jnp.broadcast_to(table_heads[:, NB - 1][:, None, None], (heads, SPAN, 1))
    ext = jnp.concatenate([body, last], axis=2).reshape(heads * SPAN, SPAN + 1)
    full = dot(ext, column_classes().astype(BF), 1, 1)
    full = full.reshape(heads, SPAN, 32, 32).transpose(0, 2, 1, 3).reshape(heads, 32, SPAN * 32)
    return jnp.pad(full, ((0, 0), (0, 0), (0, EW - SPAN * 32)))


def gather_table_grad(acc):
    heads = acc.shape[0]
    pairs = acc[:, :, : SPAN * 32].reshape(heads, 32, SPAN, 32).transpose(0, 2, 1, 3)
    sums = lax.dot_general(
        pairs.reshape(heads * SPAN, 1024),
        column_classes().astype(F32),
        (((1,), (0,)), ((), ())),
        precision=lax.Precision.HIGHEST,
        preferred_element_type=F32,
    ).reshape(heads, SPAN, SPAN + 1)
    body = sums[:, :, :SPAN].reshape(heads, SPAN * SPAN)
    last = jnp.sum(sums[:, :, SPAN], axis=1, keepdims=True)
    gap = jnp.zeros((heads, NB - 1 - SPAN * SPAN), F32)
    return jnp.concatenate([body, gap, last], axis=1).T


def make_local(mesh):
    pairs = [(0, 1), (1, 0)]
    world = mesh.size

    def swap(value):
        return lax.ppermute(value, "img", pairs)

    def local(inputs, flat_params, bias_table, bucket_index, valid_mask, cotangent):
        rows = inputs.shape[1]
        me = lax.axis_index("img")
        stream = inputs[0]
        grad_out = cotangent[0]
        grad_out_b = grad_out.astype(BF)

        table_full = lax.all_gather(bias_table, ("img", "dp"), axis=0, tiled=True)
        flat_full = lax.all_gather(flat_params, ("img", "dp"), axis=0, tiled=True)

        place = slot_places(bucket_index)
        iota = jnp.arange(LP)[:, None]
        here = (place[None, :] == iota)
        valid = valid_mask[0].astype(F32)
        pen = jnp.sum(jnp.where(here, -PENALTY * (1.0 - valid)[None, :], 0.0), axis=1)
        pen = jnp.where(jnp.any(here, axis=1), pen, ABSENT)
        pen = jnp.broadcast_to(pen[:, None], (LP, 128))
        own_place = lax.dynamic_slice_in_dim(place, me * rows, rows, 0)
        far_place = lax.dynamic_slice_in_dim(place, (1 - me) * rows, rows, 0)
        perm_own = (own_place[None, :] == iota).astype(BF)
        perm_far = (far_place[None, :] == iota).astype(BF)

        own_table = lax.dynamic_slice_in_dim(table_full, me * HL, HL, 1)
        bias = spread_table(own_table.T)

        vec = flat_full[D_END : D_END + VECTORS].astype(F32)
        n1_gain, n1_shift, b_query, b_value, b_out, n2_gain, n2_shift, b_down = (
            vec[i * D : (i + 1) * D] for i in range(8)
        )
        b_up = jnp.pad(vec[8 * D :], (0, FFP - FF)).reshape(1, FFP)
        w_qkv = flat_full[:Q_END].reshape(D, 3 * D)
        half = D // 2
        w_half = jnp.concatenate(
            [lax.dynamic_slice_in_dim(w_qkv, i * D + me * half, half, 1) for i in range(3)], axis=1
        )
        w_out = flat_full[Q_END:O_END].reshape(D, D)
        w_up = jnp.pad(flat_full[O_END:U_END].reshape(D, FF), ((0, 0), (0, FFP - FF)))
        w_down = jnp.pad(flat_full[U_END:D_END].reshape(FF, D), ((0, FFP - FF), (0, 0)))
        own_bias = jnp.concatenate(
            [
                lax.dynamic_slice_in_dim(b_query, me * half, half, 0),
                jnp.zeros((half,), F32),
                lax.dynamic_slice_in_dim(b_value, me * half, half, 0),
            ]
        )

        attn_full, normed1, inv_std1 = layer_norm(stream, n1_gain, n1_shift)
        attn_in = attn_full.astype(BF)
        attn_far = swap(attn_in)
        x_grid = (dot(perm_own, attn_in, 1, 0) + dot(perm_far, attn_far, 1, 0)).astype(BF)
        qkv = (dot(w_half, x_grid, 0, 1) + own_bias[:, None]).astype(BF).reshape(3, HL, DH, LP)
        mixed_t, log_norm = run_forward(qkv, bias, pen)
        mixed_t = mixed_t.reshape(half, LP)
        mixed_far = swap(dot(perm_far, mixed_t, 0, 1).astype(BF))
        mixed_own = dot(perm_own, mixed_t, 0, 1).astype(BF)
        mixed = jnp.where(
            me == 0,
            jnp.concatenate([mixed_own, mixed_far], axis=1),
            jnp.concatenate([mixed_far, mixed_own], axis=1),
        )
        resid = stream + dot(mixed, w_out, 1, 0) + b_out
        mlp_full, normed2, inv_std2 = layer_norm(resid, n2_gain, n2_shift)
        mlp_in = mlp_full.astype(BF)
        mlp_out, g_mlp_in, g_up, g_down, g_b_up = run_mlp(mlp_in, grad_out_b, w_up, w_down, b_up)
        output = resid + mlp_out + b_down
        g_b_down = jnp.sum(grad_out, axis=0)
        resid_part, g_n2_gain, g_n2_shift = norm_back(g_mlp_in, normed2, inv_std2, n2_gain)
        grad_resid = grad_out + resid_part
        grad_resid_b = grad_resid.astype(BF)
        g_out = dot(mixed, grad_resid_b, 0, 0).astype(BF)
        g_b_out = jnp.sum(grad_resid, axis=0)
        w_out_own = lax.dynamic_slice_in_dim(w_out, me * half, half, 0)
        w_out_far = lax.dynamic_slice_in_dim(w_out, (1 - me) * half, half, 0)
        d_far = swap(dot(w_out_far, grad_resid_b, 1, 1).astype(BF))
        d_own = dot(w_out_own, grad_resid_b, 1, 1).astype(BF)
        d_mixed = (dot(d_own, perm_own, 1, 1) + dot(d_far, perm_far, 1, 1)).astype(BF)
        grads, acc, sums = run_backward(qkv, d_mixed.reshape(HL, DH, LP), bias, pen, log_norm)
        grads = grads.reshape(3 * half, LP)
        g_half = dot(x_grid, grads, 0, 1).astype(BF)
        grads_far = dot(grads, perm_far, 1, 0).astype(BF)
        back_far = swap(dot(grads_far, w_half, 0, 1).astype(BF))
        grads_own = dot(grads, perm_own, 1, 0).astype(BF)
        g_attn_in = dot(grads_own, w_half, 0, 1) + back_far.astype(F32)
        input_part, g_n1_gain, g_n1_shift = norm_back(g_attn_in, normed1, inv_std1, n1_gain)
        grad_in = grad_resid + input_part

        g_wide = jnp.zeros((D, 3, 2, half), BF)
        g_wide = lax.dynamic_update_slice(g_wide, g_half.reshape(D, 3, 1, half), (0, 0, me, 0))
        flat_grad = jnp.concatenate(
            [
                g_wide.reshape(-1),
                g_out.reshape(-1),
                g_up[:, :FF].reshape(-1),
                g_down[:FF].reshape(-1),
                jnp.zeros((PARAMS_PAD - D_END,), BF),
            ]
        )
        zeros = jnp.zeros((D,), F32)
        g_b_query = lax.dynamic_update_slice(zeros, sums[0, :, :, 0].reshape(-1), (me * half,))
        g_b_value = lax.dynamic_update_slice(zeros, sums[1, :, :, 0].reshape(-1), (me * half,))
        vector_grad = jnp.concatenate(
            [
                g_n1_gain, g_n1_shift, g_b_query, g_b_value, g_b_out, g_n2_gain, g_n2_shift,
                g_b_down, g_b_up[0, :FF], jnp.zeros((VEC_PAD - VECTORS,), F32),
            ]
        )
        table_grad = lax.dynamic_update_slice(
            jnp.zeros((NB, H), F32), gather_table_grad(acc), (0, me * HL)
        )
        small = jnp.concatenate(
            [vector_grad.reshape(world, -1), table_grad.reshape(world, -1)], axis=1
        )
        owned_small = lax.psum_scatter(small, ("img", "dp"), scatter_dimension=0, tiled=True)[0]
        owned_flat = lax.psum_scatter(flat_grad, ("img", "dp"), scatter_dimension=0, tiled=True)
        own_vec = VEC_PAD // world
        return (
            output[None],
            grad_in[None],
            owned_flat.astype(F32),
            owned_small[:own_vec],
            owned_small[own_vec:].reshape(NB // world, H),
        )

    return local


def solution(mesh):
    placed = (
        P("dp", "img", None),
        P(("img", "dp")),
        P(("img", "dp"), None),
        P(),
        P("dp", None),
        P("dp", "img", None),
    )
    return jax.shard_map(
        make_local(mesh),
        mesh=mesh,
        in_specs=placed,
        out_specs=(
            P("dp", "img", None),
            P("dp", "img", None),
            P(("img", "dp")),
            P(("img", "dp")),
            P(("img", "dp"), None),
        ),
        check_vma=False,
    )
```

time: 4390 us -> 1790 us (0.41)
  other arithmetic: 1810 us -> 205 us
  local copies, waits for them, and re-layouts: 1440 us -> 495 us
  matrix products: 178 us -> 64.6 us
  Pallas kernels: 0 us -> 92 us
  waiting for transfers between devices: 895 us -> 839 us
    scatter-add x1 -> x0, other arithmetic: 1580 us -> none  [head_segments(): jax.ops.segment_sum(head_scores, flat_local, num_segments=bucket_rows)]
    gather x2 -> x0, local copies, waits for them, and re-layouts: 1060 us -> none  [local(): bias_terms = jnp.take(table_heads, local_buckets, axis=1)]
    unnamed x7 -> x5, waiting for transfers between devices: 895 us -> 581 us
    all_gather x2 -> x1, waiting for transfers between devices: 0.02 us -> 259 us  [local(): flat_full = lax.all_gather(flat_params, ('img', 'dp'), axis=0, tiled=True)]
    dynamic_update_slice x0 -> x4, local copies, waits for them, and re-layouts: none -> 137 us  [the longest x1 129 us: local(): lax.dynamic_update_slice(g_wide, g_half.reshape(D, 3, 1, half), (0, 0, me...]
    dot_general x18 -> x15, matrix products: 178 us -> 64.6 us  [the longest x14 59 us: dot(): lax.dot_general(a, b, (((ca,), (cb,)), ((), ())), preferred_element_type=...]
    pallas_call x0 -> x3, Pallas kernels: none -> 92 us  [the longest x1 47.8 us: run_mlp(): pl.pallas_call(mlp_body, grid=(FFP // FB,), in_specs=[whole((rows, D)), w...]
    reshape x10 -> x16, local copies, waits for them, and re-layouts: 203 us -> 155 us  [the longest x1 22.7 us: local(): g_up[:, :FF].reshape(-1)]
  transfers between devices with their start and end apart: 5 -> 7, of which waited for: 2 -> 3; matrix products, arithmetic and copies ran while one was open for 68% -> 25% of each run, Pallas kernels for 0% -> 0%
where the time goes in v1:
time: 1790 us; the launch traced here: 1760 us
  waiting for transfers between devices  839 us (47%)
  local copies, waits for them, and re-layouts  495 us (28%)
  other arithmetic  205 us (11%)
  Pallas kernels  92 us (5%)
  matrix products  64.6 us (4%)
  blocking collectives  44.8 us (3%)
    unnamed x5, waiting for transfers between devices  581 us
    all_gather x1, waiting for transfers between devices, local(): flat_full = lax.all_gather(flat_params, ('img', 'dp'), axis=0, tiled=True)  259 us
    all_gather x1, other arithmetic, local(): flat_full = lax.all_gather(flat_params, ('img', 'dp'), axis=0, tiled=True)  177 us
    dynamic_update_slice x1, local copies, waits for them, and re-layouts, local(): lax.dynamic_update_slice(g_wide, g_half.reshape(D, 3, 1, half), (0, 0, me...  129 us
    unnamed x80, local copies, waits for them, and re-layouts  110 us
    dot_general x14, matrix products, dot(): lax.dot_general(a, b, (((ca,), (cb,)), ((), ())), preferred_element_type=...  59 us
    pallas_call x1, Pallas kernels, run_mlp(): pl.pallas_call(mlp_body, grid=(FFP // FB,), in_specs=[whole((rows, D)), w...  47.8 us
    all_gather x1, blocking collectives, local(): table_full = lax.all_gather(bias_table, ('img', 'dp'), axis=0, tiled=True)  44.8 us
  transfers between devices with their start and end apart: 7, of which 3 were waited for; matrix products, arithmetic and copies ran while one was open for 25% of the time, Pallas kernels for 0%

profile of v1, /device:TPU:0, one launch (start us, length us, event | category | flops | bytes accessed | tf_op | source)
XLA Modules:
  0.0 1760.4 jit_solution(6613269254991023821)
XLA Ops:
  7.2 10.6 reshape.274
  18.0 44.8 %all-gather.1 = bf16[32,88,16]{1,2,0:T(8,128)(2,1)S(1)} all-gather(bf16[1,88,16]{1,2,0:T(8,128)(2,1)S(1)} %bitcast.85), channel_id=1, replica_groups=mesh['img'=2,'dp'=16] {'img','dp'}, dimensions={0}, use_global_device_ids=true | all-gather | bytes 92928 | tf_op jit(solution)/shard_map/all_gather | solution.py:363
  89.5 258.6 %all-gather.4.cloned.1.call-done = bf16[32,1,476672]{2,1,0:T(2,128)(2,1)} async-done(((bf16[1,1,476672]{2,1,0:T(2,128)(2,1)}), bf16[32,1,476672]{2,1,0:T(2,128)(2,1)}) %all-gather.4.cloned.1.call-update) | async-done | bytes 30507024 | tf_op jit(solution)/shard_map/all_gather | solution.py:364
  348.1 177.1 %reduce.3 = bf16[32,476672]{1,0:T(8,128)(2,1)} reduce(bf16[32,1,476672]{2,1,0:T(2,128)(2,1)} %all-gather.4.cloned.1.call-done, bf16[]{:T(256)} %constant.171), dimensions={1}, to_apply=%all-gather.reduce_sub_computation | reduce | bytes 61014016 | tf_op jit(solution)/shard_map/all_gather | solution.py:364
  525.2 70.4 %reshape.275 = bf16[15253504]{0:T(1024)(128)(2,1)} reshape(bf16[32,476672]{1,0:T(8,128)(2,1)} %reduce.3) | data formatting | bytes 61014016
  607.7 15.2 reshape.254
  649.3 14.7 attend_forward.1
  666.0 15.1 fusion.85
  690.2 20.1 %reshape.259 = bf16[1152,4304]{1,0:T(8,128)(2,1)} reshape(bf16[4958208]{0:T(1024)(128)(2,1)} %get-tuple-element.60) | data formatting | bytes 19832832 | tf_op jit(solution)/shard_map/reshape | solution.py:392
  710.3 19.3 %reshape.260 = bf16[4304,1152]{1,0:T(8,128)(2,1)} reshape(bf16[4958208]{0:T(1024)(128)(2,1)} %get-tuple-element.59) | data formatting | bytes 19832832 | tf_op jit(solution)/shard_map/reshape | solution.py:393
  737.9 8.3 pad.18.down_ref
  758.3 47.8 %mlp_both_ways.1 = (f32[384,1152]{1,0:T(8,128)S(1)}, f32[384,1152]{1,0:T(8,128)}, bf16[1152,4352]{1,0:T(8,128)(2,1)}, bf16[4352,1152]{1,0:T(8,128)(2,1)}, f32[1,4352]{1,0:T(1,128)S(1)}) custom-call(bf16[384,1152]{1,0:T(8,128)(2,1)S(1)} %copy-done.3, bf16[1152,384]{1,0:T(8,128)(2,1)S(1)} %copy.45.xt_ref, bf16[384,1152]{1,0:T(8,128)(2,1)S(1)} %copy-done.2, ...), custom_call_target="tpu_custom_call" | custom-call | flops 23102226432 | bytes 52428800 | tf_op jit(solution)/shard_map/mlp_both_ways/pallas_call | solution.py:255
  823.5 22.7 %reshape.267 = bf16[4958208]{0:T(1024)(128)(2,1)} reshape(bf16[1152,4304]{1,0:T(8,128)(2,1)} %bitcast.80) | data formatting | bytes 19832832 | tf_op jit(solution)/shard_map/reshape | solution.py:448
  854.5 18.7 %reshape.268 = bf16[4958208]{0:T(1024)(128)(2,1)} reshape(bf16[4304,1152]{1,0:T(8,128)(2,1)} %slice.99) | data formatting | bytes 19832832 | tf_op jit(solution)/shard_map/reshape | solution.py:449
  880.3 29.4 %attend_backward.1 = (bf16[3,8,72,896]{3,2,1,0:T(8,128)(2,1)}, f32[8,32,1792]{2,1,0:T(8,128)S(1)}, f32[2,8,72,128]{3,2,1,0:T(8,128)S(1)}) custom-call(bf16[3,8,72,896]{3,2,1,0:T(8,128)(2,1)} %bitcast.91, bf16[3,8,72,896]{3,2,1,0:T(8,128)(2,1)} %bitcast.92, bf16[3,8,72,896]{3,2,1,0:T(8,128)(2,1)} %bitcast.93, bf16[8,72,896]{2,1,0:T(8,128)(2,1)S(1)} %bitcast.73, ...), custom_call_target="tpu_custom_call" | custom-call | flops 8220835840 | bytes 16777216 | tf_op jit(solution)/shard_map/attend_backward/pallas_call | solution.py:182
  911.0 8.5 convolution_convert_fusion.2
  919.5 8.7 convolution_convert_fusion
  928.7 18.3 %copy.46 = bf16[1152,3,1,576]{3,2,1,0:T(2,128)(2,1)} copy(bf16[1152,3,1,576]{0,3,1,2:T(8,128)(2,1)} %bitcast.81) | data formatting | bytes 7962624 | tf_op jit(solution)/shard_map/reshape | solution.py:443
  952.8 129.5 %dynamic_update_slice.12 = bf16[1152,3,2,576]{3,2,1,0:T(2,128)(2,1)} dynamic-update-slice(bf16[1152,3,2,576]{3,2,1,0:T(2,128)(2,1)} %broadcast_in_dim.117, bf16[1152,3,1,576]{3,2,1,0:T(2,128)(2,1)} %copy.46, s32[]{:T(128)} %constant.122.clone.1, s32[]{:T(128)} %constant.122.clone.1, s32[]{:T(128)S(6)} %select_n.167, s32[]{:T(128)} %constant.122.clone.1) | dynamic-update-slice | bytes 7962628 | tf_op jit(solution)/shard_map/dynamic_update_slice | solution.py:443
  1082.3 16.0 reshape.265
  1107.0 10.4 constant_dynamic-update-slice_fusion.1
  1151.4 9.1 multiply_reduce_fusion.1
  1166.9 118.2 %all-reduce.11.cloned.1.call-done = f32[32,1920]{1,0:T(8,128)} async-done(((f32[32,1920]{1,0:T(8,128)}), f32[32,1920]{1,0:T(8,128)}) %all-reduce.11.cloned.1.call-update) | async-done | bytes 245776
  1288.0 462.5 %all-reduce.9.cloned.1.call-done = bf16[15253504]{0:T(1024)(128)(2,1)} async-done(((bf16[15253504]{0:T(1024)(128)(2,1)}), bf16[15253504]{0:T(1024)(128)(2,1)}) %all-reduce.9.cloned.1.call-update) | async-done | bytes 30507024
  (189 shorter events, 191.7 us)
Async XLA Ops:
  7.2 10.8 copy-start.29
  7.2 341.0 %all-gather.4.cloned.1.call-start = ((), (), s32[]{:S(2)}) async-start(), calls=%async_computation | async-start | bytes 62920704 | tf_op jit(solution)/shard_map/all_gather | solution.py:364
  17.9 1267.2 %all-reduce.11.cloned.1.call-start = ((), (), s32[]{:S(2)}) async-start(), calls=%async_computation.2 | async-start | bytes 491520
  73.0 5.8 copy-start.6
  80.7 6.5 copy-start.14
  89.2 507.2 %copy-start.24 = (f32[384]{0:T(512)}, f32[384]{0:T(512)S(1)}, u32[]{:S(2)}) copy-start(f32[384]{0:T(512)S(1)} %broadcast_multiply_fusion.5) | copy-start | bytes 4612
  89.5 506.9 %copy-start.26 = (f32[384]{0:T(512)}, f32[384]{0:T(512)S(1)}, u32[]{:S(2)}) copy-start(f32[384]{0:T(512)S(1)} %add_rsqrt_fusion.1) | copy-start | bytes 4612
  596.4 87.6 %copy-start.20 = (f32[13520]{0:T(1024)}, f32[13520]{0:T(1024)S(1)}, u32[]{:S(2)}) copy-start(f32[13520]{0:T(1024)S(1)} %slice_convert_fusion) | copy-start | bytes 162244
  596.4 11.3 copy-start.21
  599.2 40.7 %collective-permute-start = (bf16[384,1152]{1,0:T(8,128)(2,1)}, bf16[384,1152]{1,0:T(8,128)(2,1)}, u32[]{:S(2)}, u32[]{:S(2)}) collective-permute-start(bf16[384,1152]{1,0:T(8,128)(2,1)} %add_convert_fusion.3), channel_id=1, source_target_pairs={{0,16},{16,0},{1,17},{17,1},{2,18},{18,2},{3,19},{19,3},{4,20},{20... | collective-permute-start | bytes 2654216 | tf_op jit(solution)/shard_map/ppermute | solution.py:354
  642.5 6.5 copy-start.18
  665.5 81.5 %collective-permute-start.1 = (bf16[384,576]{0,1:T(8,128)(2,1)}, bf16[384,576]{0,1:T(8,128)(2,1)}, u32[]{:S(2)}, u32[]{:S(2)}) collective-permute-start(bf16[384,576]{0,1:T(8,128)(2,1)} %fusion.25), channel_id=1, source_target_pairs={{0,16},{16,0},{1,17},{17,1},{2,18},{18,2},{3,19},{19,3},{4,20},{20... | collective-permute-start | bytes 1327112 | tf_op jit(solution)/shard_map/ppermute | solution.py:354
  737.9 8.3 slice-start.3
  758.3 47.8 %copy-start.5 = (f32[384,1152]{1,0:T(8,128)S(1)}, f32[384,1152]{1,0:T(8,128)}, u32[]{:S(2)}) copy-start(f32[384,1152]{1,0:T(8,128)} %copy-done.4) | copy-start | bytes 5308420
  811.5 66.4 %collective-permute-start.2 = (bf16[576,384]{1,0:T(8,128)(2,1)S(1)}, bf16[576,384]{1,0:T(8,128)(2,1)S(1)}, u32[]{:S(2)}, u32[]{:S(2)}) collective-permute-start(bf16[576,384]{1,0:T(8,128)(2,1)S(1)} %fusion.21), channel_id=1, source_target_pairs={{0,16},{16,0},{1,17},{17,1},{2,18},{18,2},{3,19},{19,3},{4,20},{20... | collective-permute-start | bytes 1327112 | tf_op jit(solution)/shard_map/ppermute | solution.py:354
  911.0 8.5 copy-start.19
  928.3 223.1 %collective-permute-start.3 = (bf16[384,1152]{1,0:T(8,128)(2,1)}, bf16[384,1152]{1,0:T(8,128)(2,1)}, u32[]{:S(2)}, u32[]{:S(2)}) collective-permute-start(bf16[384,1152]{1,0:T(8,128)(2,1)} %convolution_convert_fusion.2), channel_id=1, source_target_pairs={{0,16},{16,0},{1,17},{17,1},{2,18},{18,2},{3,19},{19,3},{4,20},{20... | collective-permute-start | bytes 2654216 | tf_op jit(solution)/shard_map/ppermute | solution.py:354
  1098.3 7.2 copy-start.12
  1105.5 11.9 slice-start
  1107.0 10.4 slice-start.1
  1107.0 10.4 slice-start.2
  1126.5 6.8 copy-start.28
  1151.4 9.1 copy-start.23
  1161.4 589.1 %all-reduce.9.cloned.1.call-start = ((), (), s32[]{:S(2)}) async-start(), calls=%async_computation.1 | async-start | bytes 61014016
  (20 other events, 48.7 us)
Sparse Core Ops, SparseCore 0:
  18.0 330.0 all-gather.3
  1161.5 123.5 all-reduce.10
  1291.5 458.9 all-reduce.8

commit v2 on v1

--- a/solution.py
+++ b/solution.py
@@ -346,6 +346,298 @@
     return jnp.concatenate([body, gap, last], axis=1).T
 
 
+TQ, TO, TU, TD = 0, 3888, 5184, 10026
+TEND = 14868
+TILES = 14896
+GRAD_TILES = TD + 17 * 288
+
+def tile_spec(count, start):
+    return pl.BlockSpec((pl.Element(count), pl.Element(8), pl.Element(128)), lambda g, *_: (start + g * count, 0, 0))
+
+def lanes(rows):
+    return lax.broadcasted_iota(jnp.int32, (rows, 128), 1)
+
+def load_flat(ref, scr):
+    n = ref.shape[0]
+    scr[...] = ref[...].astype(F32).reshape(n * 8, 128)
+
+def store_flat(ref, scr):
+    n = ref.shape[0]
+    ref[...] = scr[...].reshape(n, 8, 128).astype(BF)
+
+def qkv_in_body(me_ref, ref, out, scr):
+    load_flat(ref, scr)
+    rows = out.shape[0]
+    lane = lanes(rows)
+    def go(me):
+        def half(u):
+            v = 18 * (u // 9) + 9 * me + u % 9
+            x = scr[pl.ds(v // 2, rows, stride=27), :]
+            return x if v % 2 == u % 2 else pltpu.roll(x, 64, 1)
+        for J in range(13):
+            out[:, J * 128:(J + 1) * 128] = jnp.where(lane < 64, half(2 * J), half(2 * J + 1)).astype(BF)
+        out[:, 13 * 128:] = half(26)[:, :64].astype(BF)
+    pl.when(me_ref[0] == 0)(lambda: go(0))
+    pl.when(me_ref[0] == 1)(lambda: go(1))
+
+def qkv_out_body(me_ref, x_ref, *rest):
+    ref, scr = rest[-2:]
+    rows = x_ref.shape[0]
+    lane = lanes(rows)
+    def go(me):
+        def half(v, side):
+            i, w = v // 18, v % 18
+            if w // 9 != me:
+                return jnp.zeros((rows, 128), F32)
+            u = 9 * i + w % 9
+            if u == 26:
+                x = jnp.concatenate([x_ref[:, 13 * 128:], x_ref[:, 13 * 128:]], axis=1).astype(F32)
+                return x
+            x = x_ref[:, (u // 2) * 128:(u // 2) * 128 + 128].astype(F32)
+            return x if u % 2 == side else pltpu.roll(x, 64, 1)
+        for J in range(27):
+            scr[pl.ds(J, rows, stride=27), :] = jnp.where(lane < 64, half(2 * J, 0), half(2 * J + 1, 1))
+    pl.when(me_ref[0] == 0)(lambda: go(0))
+    pl.when(me_ref[0] == 1)(lambda: go(1))
+    store_flat(ref, scr)
+
+def plain_in_body(last, ref, out, scr):
+    load_flat(ref, scr)
+    rows = out.shape[0]
+    def go(shift, count):
+        for j in range(9):
+            x = scr[pl.ds(shift + j, count, stride=9), :].astype(BF)
+            if count < rows:
+                x = jnp.concatenate([x, jnp.zeros((rows - count, 128), BF)], axis=0)
+            out[:, j * 128:(j + 1) * 128] = x
+    if last is None:
+        go(0, rows)
+    else:
+        g = pl.program_id(0)
+        pl.when(g < pl.num_programs(0) - 1)(lambda: go(0, rows))
+        pl.when(g == pl.num_programs(0) - 1)(lambda: go(*last))
+
+def plain_out_body(x_ref, *rest):
+    ref, scr = rest[-2:]
+    rows = x_ref.shape[0]
+    for j in range(9):
+        scr[pl.ds(j, rows, stride=9), :] = x_ref[:, j * 128:(j + 1) * 128].astype(F32)
+    store_flat(ref, scr)
+
+def up_in_body(ref, out, scr, wide):
+    load_flat(ref, scr)
+    lane = lanes(8)
+    for p in range(8):
+        k0, o = divmod(FF * p, 128)
+        prev = None
+        for j in range(35):
+            if k0 + j < 269:
+                x = scr[pl.ds(k0 + j, 8, stride=269), :]
+                if o:
+                    x = pltpu.roll(x, 128 - o, 1)
+            if j > 0:
+                blk = prev if o == 0 else jnp.where(lane < 128 - o, prev, x)
+                wide[j - 1, pl.ds(p, 8, stride=8), :] = blk
+            prev = x
+    for j in range(34):
+        out[:, j * 128:(j + 1) * 128] = wide[j].astype(BF)
+
+def up_out_body(x_ref, *rest):
+    ref, scr, wide = rest[-3:]
+    for j in range(34):
+        wide[j] = x_ref[:, j * 128:(j + 1) * 128].astype(F32)
+    lane = lanes(8)
+    carry = None
+    for p in range(8):
+        k0, o = divmod(FF * p, 128)
+        k1, e = divmod(FF * (p + 1), 128)
+        prev = carry
+        for j in range(k1 - k0 + 1):
+            if j < 34:
+                x = wide[j, pl.ds(p, 8, stride=8), :]
+                if o:
+                    x = pltpu.roll(x, o, 1)
+            cur = x if o == 0 else jnp.where(lane < o, prev, x)
+            if k0 + j < k1:
+                scr[pl.ds(k0 + j, 8, stride=269), :] = cur
+            else:
+                carry = cur
+            prev = x
+    store_flat(ref, scr)
+
+PARAMS = pltpu.CompilerParams(vmem_limit_bytes=40 * 2**20)
+
+def scr_of(count):
+    return pltpu.VMEM((count * 8, 128), F32)
+
+def qkv_in(flat, me):
+    return pl.pallas_call(
+        qkv_in_body,
+        grid_spec=pltpu.PrefetchScalarGridSpec(num_scalar_prefetch=1, grid=(12,),
+            in_specs=[tile_spec(324, TQ)], out_specs=pl.BlockSpec((96, 1728), lambda g, *_: (g, 0)),
+            scratch_shapes=[scr_of(324)]),
+        out_shape=jax.ShapeDtypeStruct((D, 1728), BF), compiler_params=PARAMS, name="qkv_in")(me, flat)
+
+def out_in(flat):
+    return pl.pallas_call(
+        lambda *r: plain_in_body(None, *r), grid=(9,), in_specs=[tile_spec(144, TO)],
+        out_specs=pl.BlockSpec((128, D), lambda g: (g, 0)), scratch_shapes=[scr_of(144)],
+        out_shape=jax.ShapeDtypeStruct((D, D), BF), compiler_params=PARAMS, name="out_in")(flat)
+
+def up_in(flat):
+    return pl.pallas_call(
+        up_in_body, grid=(18,), in_specs=[tile_spec(269, TU)],
+        out_specs=pl.BlockSpec((64, FFP), lambda g: (g, 0)), scratch_shapes=[scr_of(269), pltpu.VMEM((34, 64, 128), F32)],
+        out_shape=jax.ShapeDtypeStruct((D, FFP), BF), compiler_params=PARAMS, name="up_in")(flat)
+
+def down_in(flat):
+    spec = pl.BlockSpec((pl.Element(288), pl.Element(8), pl.Element(128)), lambda g: (jnp.minimum(TD + g * 288, TILES - 288), 0, 0))
+    return pl.pallas_call(
+        lambda *r: plain_in_body((208, 208), *r), grid=(17,), in_specs=[spec],
+        out_specs=pl.BlockSpec((256, D), lambda g: (g, 0)), scratch_shapes=[scr_of(288)],
+        out_shape=jax.ShapeDtypeStruct((FFP, D), BF), compiler_params=PARAMS, name="down_in")(flat)
+
+GRAD = jax.ShapeDtypeStruct((GRAD_TILES, 8, 128), BF)
+ANY = pl.BlockSpec(memory_space=pl.ANY)
+
+def down_out(x):
+    return pl.pallas_call(
+        plain_out_body, grid=(17,), in_specs=[pl.BlockSpec((256, D), lambda g: (g, 0))],
+        out_specs=tile_spec(288, TD), scratch_shapes=[scr_of(288)],
+        out_shape=GRAD, compiler_params=PARAMS, name="down_out")(x)
+
+def up_out(x, flat):
+    return pl.pallas_call(
+        up_out_body, grid=(18,), in_specs=[pl.BlockSpec((64, FFP), lambda g: (g, 0)), ANY],
+        out_specs=tile_spec(269, TU), scratch_shapes=[scr_of(269), pltpu.VMEM((34, 64, 128), F32)],
+        input_output_aliases={1: 0},
+        out_shape=GRAD, compiler_params=PARAMS, name="up_out")(x, flat)
+
+def out_out(x, flat):
+    return pl.pallas_call(
+        plain_out_body, grid=(9,), in_specs=[pl.BlockSpec((128, D), lambda g: (g, 0)), ANY],
+        out_specs=tile_spec(144, TO), scratch_shapes=[scr_of(144)], input_output_aliases={1: 0},
+        out_shape=GRAD, compiler_params=PARAMS, name="out_out")(x, flat)
+
+def qkv_out(x, flat, me):
+    return pl.pallas_call(
+        qkv_out_body,
+        grid_spec=pltpu.PrefetchScalarGridSpec(num_scalar_prefetch=1, grid=(12,),
+            in_specs=[pl.BlockSpec((96, 1728), lambda g, *_: (g, 0)), ANY], out_specs=tile_spec(324, TQ),
+            scratch_shapes=[scr_of(324)]),
+        input_output_aliases={2: 0},
+        out_shape=GRAD, compiler_params=PARAMS, name="qkv_out")(me, x, flat)
+
+
+TILE = 1024
+
+
+class Net:
+    def __init__(self, mesh):
+        self.dp = mesh.shape["dp"]
+        self.chips = mesh.size // 2
+        half = self.chips // 2
+        bits = [1 << i for i in range(half.bit_length() - 1)]
+        x, zs, y = bits[0], bits[1:], half
+        self.orders = (zs + [x, y], zs + [y, x])
+        self.stages = len(self.orders[0])
+        self.core_pairs = [(d, d ^ 1) for d in range(mesh.size)]
+
+    def stage_pairs(self, s):
+        return [
+            (2 * q + c, 2 * (q ^ self.orders[c][s]) + c) for q in range(self.chips) for c in (0, 1)
+        ]
+
+    def send(self, value, pairs):
+        return lax.ppermute(value, ("img", "dp"), pairs)
+
+    def mask(self, b, c):
+        total = 0
+        for s in range(self.stages):
+            if b >> s & 1:
+                total ^= self.orders[c][s]
+        return total
+
+    def place(self):
+        me = lax.axis_index("img") * self.dp + lax.axis_index("dp")
+        return me // 2, me % 2
+
+    def offsets(self, tiles):
+        chip, core = self.place()
+        masks = jnp.array(
+            [[self.mask(b, c) for b in range(self.chips)] for c in (0, 1)], jnp.int32
+        )
+        step = (tiles - 1) // 2
+        own = (chip ^ masks[core]) * tiles + core * step
+        far = (chip ^ masks[1 - core]) * tiles + (1 - core) * step
+        return own, far
+
+
+def unfilled(shape):
+    return pl.pallas_call(
+        lambda ref: None,
+        out_specs=pl.BlockSpec(memory_space=pl.ANY),
+        out_shape=jax.ShapeDtypeStruct(shape, BF),
+        name="unfilled",
+    )()
+
+
+def chip_part(net, shard):
+    _, core = net.place()
+    length = shard.shape[0]
+    gap = -length % TILE
+    got = net.send(jnp.where(core == 0, shard[length - gap :], shard[:gap]), net.core_pairs)
+    both = jnp.where(core == 0, jnp.concatenate([shard, got]), jnp.concatenate([got, shard]))
+    return both.reshape(-1, 8, 128)
+
+
+def gather_flat(net, shard):
+    tiles = 2 * shard.shape[0] // TILE
+    own = {0: chip_part(net, shard)}
+    far = {}
+    own_at, far_at = net.offsets(tiles)
+    flat = unfilled((net.chips * tiles, 8, 128))
+    for s in range(net.stages):
+        for b in range(1 << s):
+            own[b + (1 << s)] = net.send(own[b], net.stage_pairs(s))
+    for b in range(net.chips):
+        far[b] = net.send(own[b], net.core_pairs)
+        flat = lax.dynamic_update_slice(flat, own[b], (own_at[b], 0, 0))
+        flat = lax.dynamic_update_slice(flat, far[b], (far_at[b], 0, 0))
+    return flat
+
+
+def add(a, b):
+    return (a.astype(F32) + b.astype(F32)).astype(BF)
+
+
+def scatter_flat(net, flat, length):
+    tiles = 2 * length // TILE
+    half = (tiles + 1) // 2
+    own_at, far_at = net.offsets(tiles)
+    acc = {}
+    for b in reversed(range(net.chips)):
+        away = lax.dynamic_slice(flat, (far_at[b], 0, 0), (half, 8, 128))
+        came = net.send(away, net.core_pairs)
+        acc[b] = add(lax.dynamic_slice(flat, (own_at[b], 0, 0), (half, 8, 128)), came)
+    for s in reversed(range(net.stages)):
+        for b in reversed(range(1 << s)):
+            came = net.send(acc.pop(b + (1 << s)), net.stage_pairs(s))
+            acc[b] = add(acc[b], came) if s else acc[b].astype(F32) + came.astype(F32)
+    total = acc[0].reshape(-1)
+    _, core = net.place()
+    return jnp.where(core == 0, total[:length], total[half * TILE - length :])
+
+
+def gather_table(bias_table, world):
+    rows, heads = bias_table.shape
+    size = rows * heads
+    full = -(-size // TILE) * TILE
+    shard = jnp.pad(bias_table.reshape(-1), (0, full - size)).reshape(-1, 8, 128)
+    got = lax.all_gather(shard, ("img", "dp"), axis=0, tiled=True)
+    return got.reshape(world, full)[:, :size].reshape(world * rows, heads)
+
+
 def make_local(mesh):
     pairs = [(0, 1), (1, 0)]
     world = mesh.size
@@ -360,8 +652,15 @@
         grad_out = cotangent[0]
         grad_out_b = grad_out.astype(BF)
 
-        table_full = lax.all_gather(bias_table, ("img", "dp"), axis=0, tiled=True)
-        flat_full = lax.all_gather(flat_params, ("img", "dp"), axis=0, tiled=True)
+        shard = flat_params.shape[0]
+        paired = (2 * shard) % TILE == 0 and mesh.size & (mesh.size - 1) == 0
+        net = Net(mesh) if paired else None
+        if paired:
+            flat_full = gather_flat(net, flat_params)
+        else:
+            flat_full = lax.all_gather(flat_params, ("img", "dp"), axis=0, tiled=True)
+            flat_full = flat_full.reshape(TILES, 8, 128)
+        table_full = gather_table(bias_table, world)
 
         place = slot_places(bucket_index)
         iota = jnp.arange(LP)[:, None]
@@ -378,19 +677,16 @@
         own_table = lax.dynamic_slice_in_dim(table_full, me * HL, HL, 1)
         bias = spread_table(own_table.T)
 
-        vec = flat_full[D_END : D_END + VECTORS].astype(F32)
+        vec = flat_full[TEND : TEND + 14].reshape(-1)[:VECTORS].astype(F32)
         n1_gain, n1_shift, b_query, b_value, b_out, n2_gain, n2_shift, b_down = (
             vec[i * D : (i + 1) * D] for i in range(8)
         )
         b_up = jnp.pad(vec[8 * D :], (0, FFP - FF)).reshape(1, FFP)
-        w_qkv = flat_full[:Q_END].reshape(D, 3 * D)
         half = D // 2
-        w_half = jnp.concatenate(
-            [lax.dynamic_slice_in_dim(w_qkv, i * D + me * half, half, 1) for i in range(3)], axis=1
-        )
-        w_out = flat_full[Q_END:O_END].reshape(D, D)
-        w_up = jnp.pad(flat_full[O_END:U_END].reshape(D, FF), ((0, 0), (0, FFP - FF)))
-        w_down = jnp.pad(flat_full[U_END:D_END].reshape(FF, D), ((0, FFP - FF), (0, 0)))
+        w_half = qkv_in(flat_full, me[None])
+        w_out = out_in(flat_full)
+        w_up = up_in(flat_full)
+        w_down = down_in(flat_full)
         own_bias = jnp.concatenate(
             [
                 lax.dynamic_slice_in_dim(b_query, me * half, half, 0),
@@ -439,17 +735,10 @@
         input_part, g_n1_gain, g_n1_shift = norm_back(g_attn_in, normed1, inv_std1, n1_gain)
         grad_in = grad_resid + input_part
 
-        g_wide = jnp.zeros((D, 3, 2, half), BF)
-        g_wide = lax.dynamic_update_slice(g_wide, g_half.reshape(D, 3, 1, half), (0, 0, me, 0))
-        flat_grad = jnp.concatenate(
-            [
-                g_wide.reshape(-1),
-                g_out.reshape(-1),
-                g_up[:, :FF].reshape(-1),
-                g_down[:FF].reshape(-1),
-                jnp.zeros((PARAMS_PAD - D_END,), BF),
-            ]
-        )
+        flat_grad = down_out(g_down)
+        flat_grad = up_out(g_up, flat_grad)
+        flat_grad = out_out(g_out, flat_grad)
+        flat_grad = qkv_out(g_half, flat_grad, me[None])
         zeros = jnp.zeros((D,), F32)
         g_b_query = lax.dynamic_update_slice(zeros, sums[0, :, :, 0].reshape(-1), (me * half,))
         g_b_value = lax.dynamic_update_slice(zeros, sums[1, :, :, 0].reshape(-1), (me * half,))
@@ -466,12 +755,20 @@
             [vector_grad.reshape(world, -1), table_grad.reshape(world, -1)], axis=1
         )
         owned_small = lax.psum_scatter(small, ("img", "dp"), scatter_dimension=0, tiled=True)[0]
-        owned_flat = lax.psum_scatter(flat_grad, ("img", "dp"), scatter_dimension=0, tiled=True)
+        if paired:
+            owned_flat = scatter_flat(net, flat_grad, shard)
+        else:
+            owned_flat = lax.psum_scatter(
+                flat_grad[:TILES].reshape(-1), ("img", "dp"), scatter_dimension=0, tiled=True
+            ).astype(F32)
+        number = me * mesh.shape["dp"] + lax.axis_index("dp")
+        spot = jnp.arange(shard) + number * shard
+        owned_flat = jnp.where(spot < D_END, owned_flat, 0.0)
         own_vec = VEC_PAD // world
         return (
             output[None],
             grad_in[None],
-            owned_flat.astype(F32),
+            owned_flat,
             owned_small[:own_vec],
             owned_small[own_vec:].reshape(NB // world, H),
         )

time: 1790 us -> 929 us (0.52)
  waiting for transfers between devices: 839 us -> 287 us
  local copies, waits for them, and re-layouts: 495 us -> 136 us
  other arithmetic: 205 us -> 54.4 us
  between operations: 14.7 us -> 116 us
  Pallas kernels: 92 us -> 164 us
  starting transfers between devices: 4.15 us -> 42.3 us
    unnamed x5 -> x2, waiting for transfers between devices: 581 us -> 123 us
    all_gather x1 -> x0, waiting for transfers between devices: 259 us -> none  [local(): flat_full = lax.all_gather(flat_params, ('img', 'dp'), axis=0, tiled=True)]
    all_gather x1 -> x0, other arithmetic: 177 us -> none  [local(): flat_full = lax.all_gather(flat_params, ('img', 'dp'), axis=0, tiled=True)]
    ppermute x0 -> x63, waiting for transfers between devices: none -> 156 us  [send(): return lax.ppermute(value, ('img', 'dp'), pairs)]
    reshape x9 -> x5, local copies, waits for them, and re-layouts: 142 us -> 1.46 us  [the longest x1 0.75 us: local(): vec = flat_full[TEND:TEND + 14].reshape(-1)[:VECTORS].astype(F32)]
    unnamed x80 -> x138, local copies, waits for them, and re-layouts: 110 us -> 16 us
    dynamic_update_slice x1 -> x31, local copies, waits for them, and re-layouts: 129 us -> 48.9 us  [the longest x15 26 us: gather_flat(): flat = lax.dynamic_update_slice(flat, own[b], (own_at[b], 0, 0))]
    pallas_call x0 -> x9, Pallas kernels: none -> 72 us  [the longest x1 14.5 us: up_in(): pl.pallas_call(up_in_body, grid=(18,), in_specs=[tile_spec(269, TU)], out...]
  transfers between devices with their start and end apart: 7 -> 68, of which waited for: 3 -> 17; matrix products, arithmetic and copies ran while one was open for 25% -> 19% of each run, Pallas kernels for 0% -> 7%
where the time goes in v2:
time: 929 us; the launch traced here: 915 us
  waiting for transfers between devices  287 us (31%)
  Pallas kernels  164 us (18%)
  local copies, waits for them, and re-layouts  136 us (15%)
  between operations  116 us (12%)
  matrix products  58.7 us (6%)
  blocking collectives  56.1 us (6%)
  other arithmetic  54.4 us (6%)
  starting transfers between devices  42.3 us (5%)
    ppermute x63, waiting for transfers between devices, send(): return lax.ppermute(value, ('img', 'dp'), pairs)  156 us
    unnamed x2, waiting for transfers between devices  123 us
    all_gather x1, blocking collectives, gather_table(): got = lax.all_gather(shard, ('img', 'dp'), axis=0, tiled=True)  56.1 us
    dot_general x14, matrix products, dot(): lax.dot_general(a, b, (((ca,), (cb,)), ((), ())), preferred_element_type=...  53.1 us
    pallas_call x1, Pallas kernels, run_mlp(): pl.pallas_call(mlp_body, grid=(FFP // FB,), in_specs=[whole((rows, D)), w...  48 us
    ppermute x63, starting transfers between devices, send(): return lax.ppermute(value, ('img', 'dp'), pairs)  37.4 us
    pallas_call x1, Pallas kernels, run_backward(): pl.pallas_call(attend_backward, grid=(HL,), in_specs=[head_block(0), head...  29.4 us
    dynamic_update_slice x15, local copies, waits for them, and re-layouts, gather_flat(): flat = lax.dynamic_update_slice(flat, own[b], (own_at[b], 0, 0))  26 us
  transfers between devices with their start and end apart: 68, of which 17 were waited for; matrix products, arithmetic and copies ran while one was open for 19% of the time, Pallas kernels for 7%

profile of v2, /device:TPU:0, one launch (start us, length us, event | category | flops | bytes accessed | tf_op | source)
XLA Modules:
  0.0 915.3 jit_solution(14873731371231633493)
XLA Ops:
  16.2 56.1 %all_gather.3 = bf16[64,8,128]{2,1,0:T(8,128)(2,1)S(1)} all-gather(bf16[2,8,128]{2,1,0:T(8,128)(2,1)S(1)} %pad_bitcast_fusion), channel_id=1, replica_groups=mesh['img'=2,'dp'=16] {'img','dp'}, dimensions={0}, use_global_device_ids=true | all-gather | bytes 135168 | tf_op jit(solution)/shard_map/all_gather | solution.py:637
  80.1 35.4 %collective-permute-done.4 = bf16[466,8,128]{2,1,0:T(8,128)(2,1)} collective-permute-done((bf16[466,8,128]{2,1,0:T(8,128)(2,1)}, bf16[466,8,128]{2,1,0:T(8,128)(2,1)}, u32[]{:S(2)}, u32[]{:S(2)}) %collective-permute-start.4) | collective-permute-done | bytes 954400 | tf_op jit(solution)/shard_map/ppermute | solution.py:552
  120.7 38.0 %collective-permute-done.6 = bf16[466,8,128]{2,1,0:T(8,128)(2,1)S(1)} collective-permute-done((bf16[466,8,128]{2,1,0:T(8,128)(2,1)}, bf16[466,8,128]{2,1,0:T(8,128)(2,1)S(1)}, u32[]{:S(2)}, u32[]{:S(2)}) %collective-permute-start.6) | collective-permute-done | bytes 954400 | tf_op jit(solution)/shard_map/ppermute | solution.py:552
  287.4 10.2 %collective-permute-done.30 = bf16[466,8,128]{2,1,0:T(8,128)(2,1)S(1)} collective-permute-done((bf16[466,8,128]{2,1,0:T(8,128)(2,1)}, bf16[466,8,128]{2,1,0:T(8,128)(2,1)S(1)}, u32[]{:S(2)}, u32[]{:S(2)}) %collective-permute-start.30) | collective-permute-done | bytes 954400 | tf_op jit(solution)/shard_map/ppermute | solution.py:552
  314.2 8.6 qkv_in.1
  326.2 7.8 collective-permute-done.32
  343.3 14.8 %attend_forward.1 = (bf16[8,72,896]{2,1,0:T(8,128)(2,1)S(1)}, f32[8,1,896]{2,1,0:T(1,128)S(1)}) custom-call(bf16[3,8,72,896]{3,2,1,0:T(8,128)(2,1)} %bitcast.129, bf16[3,8,72,896]{3,2,1,0:T(8,128)(2,1)} %bitcast.130, bf16[3,8,72,896]{3,2,1,0:T(8,128)(2,1)} %bitcast.131, f32[8,32,1792]{2,1,0:T(8,128)S(1)} %pad.13.e_ref, f32[896,128]{1,0:T(8,128)S(1)} %broadcast_in_dim.117.pen_ref), custom_call_target="tpu_custom_call" | custom-call | flops 3288334336 | bytes 8388608 | tf_op jit(solution)/shard_map/attend_forward/pallas_call | solution.py:150
  389.3 14.5 %up_in.1.up_ref = bf16[1152,4352]{1,0:T(8,128)(2,1)S(1)} custom-call(bf16[14896,8,128]{2,1,0:T(8,128)(2,1)} %constant_dynamic-update-slice_fusion.ref.r_0_), custom_call_target="tpu_custom_call" | custom-call | tf_op jit(solution)/shard_map/up_in/pallas_call | solution.py:488
  407.6 12.0 %down_in.1.down_ref = bf16[4352,1152]{1,0:T(8,128)(2,1)S(1)} custom-call(bf16[14896,8,128]{2,1,0:T(8,128)(2,1)} %constant_dynamic-update-slice_fusion.ref.r_0_), custom_call_target="tpu_custom_call" | custom-call | tf_op jit(solution)/shard_map/down_in/pallas_call | solution.py:495
  431.8 48.0 %mlp_both_ways.1 = (f32[384,1152]{1,0:T(8,128)S(1)}, f32[384,1152]{1,0:T(8,128)}, bf16[1152,4352]{1,0:T(8,128)(2,1)}, bf16[4352,1152]{1,0:T(8,128)(2,1)}, f32[1,4352]{1,0:T(1,128)S(1)}) custom-call(bf16[384,1152]{1,0:T(8,128)(2,1)S(1)} %copy-done.9, bf16[1152,384]{1,0:T(8,128)(2,1)S(1)} %copy.55.xt_ref, bf16[384,1152]{1,0:T(8,128)(2,1)S(1)} %copy-done.8, ...), custom_call_target="tpu_custom_call" | custom-call | flops 23102226432 | bytes 52428800 | tf_op jit(solution)/shard_map/mlp_both_ways/pallas_call | solution.py:255
  490.9 8.7 down_out.1.rest_0_
  499.7 12.0 %up_out.1.rest_0_ = bf16[14922,8,128]{2,1,0:T(8,128)(2,1)} custom-call(bf16[1152,4352]{1,0:T(8,128)(2,1)S(1)} %bitcast.112, bf16[14922,8,128]{2,1,0:T(8,128)(2,1)} %down_out.1.rest_0_), custom_call_target="tpu_custom_call", output_to_operand_aliasing={{}: (1, {})} | custom-call | tf_op jit(solution)/shard_map/up_out/pallas_call | solution.py:510
  522.7 29.4 %attend_backward.1 = (bf16[3,8,72,896]{3,2,1,0:T(8,128)(2,1)}, f32[8,32,1792]{2,1,0:T(8,128)S(1)}, f32[2,8,72,128]{3,2,1,0:T(8,128)S(1)}) custom-call(bf16[3,8,72,896]{3,2,1,0:T(8,128)(2,1)} %bitcast.132, bf16[3,8,72,896]{3,2,1,0:T(8,128)(2,1)} %bitcast.133, bf16[3,8,72,896]{3,2,1,0:T(8,128)(2,1)} %bitcast.134, bf16[8,72,896]{2,1,0:T(8,128)(2,1)S(1)} %bitcast.116, ...), custom_call_target="tpu_custom_call" | custom-call | flops 8220835840 | bytes 16777216 | tf_op jit(solution)/shard_map/attend_backward/pallas_call | solution.py:182
  552.1 8.8 convolution_convert_fusion
  569.4 6.8 qkv_out.1
  576.2 9.7 %constant_dynamic-slice_fusion.13 = (bf16[466,8,128]{2,1,0:T(8,128)(2,1)}, bf16[466,8,128]{2,1,0:T(8,128)(2,1)}, bf16[466,8,128]{2,1,0:T(8,128)(2,1)}, bf16[466,...) fusion(bf16[14922,8,128]{2,1,0:T(8,128)(2,1)} %qkv_out.1, ...), kind=kLoop, calls=%fused_computation.137 | loop fusion | bytes 30539840 | tf_op jit(solution)/shard_map/dynamic_slice | solution.py:620
  611.2 8.8 add_convert_fusion.30
  655.8 9.1 collective-permute-done.63
  664.9 7.4 add_convert_fusion.26
  674.3 8.4 convolution_convert_fusion.2
  690.6 10.8 %dynamic_update_slice.139 = f32[2816,16]{1,0:T(8,128)S(1)} dynamic-update-slice(f32[2816,16]{1,0:T(8,128)S(1)} %broadcast_in_dim.123, f32[2816,8]{1,0:T(8,128)S(1)} %copy.60, s32[]{:T(128)} %constant.154.clone.1, s32[]{:T(128)S(6)} %select_n.434) | dynamic-update-slice | bytes 180228 | tf_op jit(solution)/shard_map/dynamic_update_slice | solution.py:751
  715.1 8.0 multiply_reduce_fusion.1
  736.5 34.8 %collective-permute-done.65 = bf16[466,8,128]{2,1,0:T(8,128)(2,1)} collective-permute-done((bf16[466,8,128]{2,1,0:T(8,128)(2,1)}, bf16[466,8,128]{2,1,0:T(8,128)(2,1)}, u32[]{:S(2)}, u32[]{:S(2)}) %collective-permute-start.65) | collective-permute-done | bytes 954400 | tf_op jit(solution)/shard_map/ppermute | solution.py:552
  777.1 122.9 %all-reduce.6.cloned.1.call-done = f32[32,1920]{1,0:T(8,128)} async-done(((f32[32,1920]{1,0:T(8,128)}), f32[32,1920]{1,0:T(8,128)}) %all-reduce.6.cloned.1.call-update) | async-done | bytes 245776
  (404 shorter events, 268.1 us)
Async XLA Ops:
  7.2 892.9 %all-reduce.6.cloned.1.call-start = ((), (), s32[]{:S(2)}) async-start(), calls=%async_computation | async-start | bytes 491520
  13.4 66.3 %collective-permute-start.2 = (bf16[466,8,128]{2,1,0:T(8,128)(2,1)}, bf16[466,8,128]{2,1,0:T(8,128)(2,1)}, u32[]{:S(2)}, u32[]{:S(2)}) collective-permute-start(bf16[466,8,128]{2,1,0:T(8,128)(2,1)} %get-tuple-element.60), channel_id=1, source_target_pairs={{0,4},{1,5},{2,6},{3,7},{4,0},{5,1},{6,2},{7,3},{8,12},{9,13},{10,... | collective-permute-start | bytes 2863112 | tf_op jit(solution)/shard_map/ppermute | solution.py:552
  72.9 42.6 %collective-permute-start.1 = (bf16[466,8,128]{2,1,0:T(8,128)(2,1)}, bf16[466,8,128]{2,1,0:T(8,128)(2,1)}, u32[]{:S(2)}, u32[]{:S(2)}) collective-permute-start(bf16[466,8,128]{2,1,0:T(8,128)(2,1)} %get-tuple-element.60), channel_id=1, source_target_pairs={{0,1},{1,0},{2,3},{3,2},{4,5},{5,4},{6,7},{7,6},{8,9},{9,8},{10,11... | collective-permute-start | bytes 2863112 | tf_op jit(solution)/shard_map/ppermute | solution.py:552
  73.3 42.2 %collective-permute-start.4 = (bf16[466,8,128]{2,1,0:T(8,128)(2,1)}, bf16[466,8,128]{2,1,0:T(8,128)(2,1)}, u32[]{:S(2)}, u32[]{:S(2)}) collective-permute-start(bf16[466,8,128]{2,1,0:T(8,128)(2,1)} %get-tuple-element.60), channel_id=1, source_target_pairs={{0,8},{1,9},{2,10},{3,11},{4,12},{5,13},{6,14},{7,15},{8,0},{9,1},... | collective-permute-start | bytes 2863112 | tf_op jit(solution)/shard_map/ppermute | solution.py:552
  115.6 43.1 %collective-permute-start.6 = (bf16[466,8,128]{2,1,0:T(8,128)(2,1)}, bf16[466,8,128]{2,1,0:T(8,128)(2,1)S(1)}, u32[]{:S(2)}, u32[]{:S(2)}) collective-permute-start(bf16[466,8,128]{2,1,0:T(8,128)(2,1)} %collective-permute-done.2), channel_id=1, source_target_pairs={{0,8},{1,9},{2,10},{3,11},{4,12},{5,13},{6,14},{7,15},{8,0},{9,1},... | collective-permute-start | bytes 2863112 | tf_op jit(solution)/shard_map/ppermute | solution.py:552
  117.8 45.1 %collective-permute-start.9 = (bf16[466,8,128]{2,1,0:T(8,128)(2,1)}, bf16[466,8,128]{2,1,0:T(8,128)(2,1)}, u32[]{:S(2)}, u32[]{:S(2)}) collective-permute-start(bf16[466,8,128]{2,1,0:T(8,128)(2,1)} %collective-permute-done.8), channel_id=1, source_target_pairs={{0,1},{1,0},{2,3},{3,2},{4,5},{5,4},{6,7},{7,6},{8,9},{9,8},{10,11... | collective-permute-start | bytes 2863112 | tf_op jit(solution)/shard_map/ppermute | solution.py:552
  118.3 45.3 %collective-permute-start.10 = (bf16[466,8,128]{2,1,0:T(8,128)(2,1)}, bf16[466,8,128]{2,1,0:T(8,128)(2,1)}, u32[]{:S(2)}, u32[]{:S(2)}) collective-permute-start(bf16[466,8,128]{2,1,0:T(8,128)(2,1)} %collective-permute-done.2), channel_id=1, source_target_pairs={{0,2},{1,17},{2,0},{3,19},{4,6},{5,21},{6,4},{7,23},{8,10},{9,25},... | collective-permute-start | bytes 2863112 | tf_op jit(solution)/shard_map/ppermute | solution.py:552
  119.0 45.9 %collective-permute-start.12 = (bf16[466,8,128]{2,1,0:T(8,128)(2,1)}, bf16[466,8,128]{2,1,0:T(8,128)(2,1)S(1)}, u32[]{:S(2)}, u32[]{:S(2)}) collective-permute-start(bf16[466,8,128]{2,1,0:T(8,128)(2,1)} %collective-permute-done.4), channel_id=1, source_target_pairs={{0,2},{1,17},{2,0},{3,19},{4,6},{5,21},{6,4},{7,23},{8,10},{9,25},... | collective-permute-start | bytes 2863112 | tf_op jit(solution)/shard_map/ppermute | solution.py:552
  120.4 44.9 %collective-permute-start.17 = (bf16[466,8,128]{2,1,0:T(8,128)(2,1)}, bf16[466,8,128]{2,1,0:T(8,128)(2,1)S(1)}, u32[]{:S(2)}, u32[]{:S(2)}) collective-permute-start(bf16[466,8,128]{2,1,0:T(8,128)(2,1)} %collective-permute-done.16), channel_id=1, source_target_pairs={{0,1},{1,0},{2,3},{3,2},{4,5},{5,4},{6,7},{7,6},{8,9},{9,8},{10,11... | collective-permute-start | bytes 2863112 | tf_op jit(solution)/shard_map/ppermute | solution.py:552
  158.7 81.7 %collective-permute-start.18 = (bf16[466,8,128]{2,1,0:T(8,128)(2,1)}, bf16[466,8,128]{2,1,0:T(8,128)(2,1)}, u32[]{:S(2)}, u32[]{:S(2)}) collective-permute-start(bf16[466,8,128]{2,1,0:T(8,128)(2,1)} %collective-permute-done.2), channel_id=1, source_target_pairs={{0,16},{1,3},{2,18},{3,1},{4,20},{5,7},{6,22},{7,5},{8,24},{9,11},... | collective-permute-start | bytes 2863112 | tf_op jit(solution)/shard_map/ppermute | solution.py:552
  162.8 82.6 %collective-permute-start.20 = (bf16[466,8,128]{2,1,0:T(8,128)(2,1)}, bf16[466,8,128]{2,1,0:T(8,128)(2,1)}, u32[]{:S(2)}, u32[]{:S(2)}) collective-permute-start(bf16[466,8,128]{2,1,0:T(8,128)(2,1)} %collective-permute-done.4), channel_id=1, source_target_pairs={{0,16},{1,3},{2,18},{3,1},{4,20},{5,7},{6,22},{7,5},{8,24},{9,11},... | collective-permute-start | bytes 2863112 | tf_op jit(solution)/shard_map/ppermute | solution.py:552
  163.6 86.2 %collective-permute-start.24 = (bf16[466,8,128]{2,1,0:T(8,128)(2,1)}, bf16[466,8,128]{2,1,0:T(8,128)(2,1)}, u32[]{:S(2)}, u32[]{:S(2)}) collective-permute-start(bf16[466,8,128]{2,1,0:T(8,128)(2,1)} %collective-permute-done.8), channel_id=1, source_target_pairs={{0,16},{1,3},{2,18},{3,1},{4,20},{5,7},{6,22},{7,5},{8,24},{9,11},... | collective-permute-start | bytes 2863112 | tf_op jit(solution)/shard_map/ppermute | solution.py:552
  165.0 85.5 %collective-permute-start.7 = (bf16[466,8,128]{2,1,0:T(8,128)(2,1)S(1)}, bf16[466,8,128]{2,1,0:T(8,128)(2,1)}, u32[]{:S(2)}, u32[]{:S(2)}) collective-permute-start(bf16[466,8,128]{2,1,0:T(8,128)(2,1)S(1)} %collective-permute-done.6), channel_id=1, source_target_pairs={{0,1},{1,0},{2,3},{3,2},{4,5},{5,4},{6,7},{7,6},{8,9},{9,8},{10,11... | collective-permute-start | bytes 2863112 | tf_op jit(solution)/shard_map/ppermute | solution.py:552
  165.3 88.4 %collective-permute-start.14 = (bf16[466,8,128]{2,1,0:T(8,128)(2,1)S(1)}, bf16[466,8,128]{2,1,0:T(8,128)(2,1)}, u32[]{:S(2)}, u32[]{:S(2)}) collective-permute-start(bf16[466,8,128]{2,1,0:T(8,128)(2,1)S(1)} %collective-permute-done.6), channel_id=1, source_target_pairs={{0,2},{1,17},{2,0},{3,19},{4,6},{5,21},{6,4},{7,23},{8,10},{9,25},... | collective-permute-start | bytes 2863112 | tf_op jit(solution)/shard_map/ppermute | solution.py:552
  360.7 60.3 %collective-permute-start.33 = (bf16[384,576]{0,1:T(8,128)(2,1)}, bf16[384,576]{0,1:T(8,128)(2,1)S(1)}, u32[]{:S(2)}, u32[]{:S(2)}) collective-permute-start(bf16[384,576]{0,1:T(8,128)(2,1)} %fusion.26), channel_id=1, source_target_pairs={{0,16},{16,0},{1,17},{17,1},{2,18},{18,2},{3,19},{19,3},{4,20},{20... | collective-permute-start | bytes 1327112 | tf_op jit(solution)/shard_map/ppermute | solution.py:646
  624.1 48.9 %collective-permute-start.43 = (bf16[466,8,128]{2,1,0:T(8,128)(2,1)}, bf16[466,8,128]{2,1,0:T(8,128)(2,1)}, u32[]{:S(2)}, u32[]{:S(2)}) collective-permute-start(bf16[466,8,128]{2,1,0:T(8,128)(2,1)} %get-tuple-element.73), channel_id=1, source_target_pairs={{0,1},{1,0},{2,3},{3,2},{4,5},{5,4},{6,7},{7,6},{8,9},{9,8},{10,11... | collective-permute-start | bytes 2863112 | tf_op jit(solution)/shard_map/ppermute | solution.py:552
  647.2 57.7 %collective-permute-start.45 = (bf16[466,8,128]{2,1,0:T(8,128)(2,1)}, bf16[466,8,128]{2,1,0:T(8,128)(2,1)}, u32[]{:S(2)}, u32[]{:S(2)}) collective-permute-start(bf16[466,8,128]{2,1,0:T(8,128)(2,1)} %get-tuple-element.83), channel_id=1, source_target_pairs={{0,16},{1,3},{2,18},{3,1},{4,20},{5,7},{6,22},{7,5},{8,24},{9,11},... | collective-permute-start | bytes 2863112 | tf_op jit(solution)/shard_map/ppermute | solution.py:552
  654.6 50.3 %collective-permute-start.60 = (bf16[466,8,128]{2,1,0:T(8,128)(2,1)}, bf16[466,8,128]{2,1,0:T(8,128)(2,1)}, u32[]{:S(2)}, u32[]{:S(2)}) collective-permute-start(bf16[466,8,128]{2,1,0:T(8,128)(2,1)} %get-tuple-element.79), channel_id=1, source_target_pairs={{0,16},{1,3},{2,18},{3,1},{4,20},{5,7},{6,22},{7,5},{8,24},{9,11},... | collective-permute-start | bytes 2863112 | tf_op jit(solution)/shard_map/ppermute | solution.py:552
  705.0 198.0 %collective-permute-start.36 = (bf16[466,8,128]{2,1,0:T(8,128)(2,1)}, bf16[466,8,128]{2,1,0:T(8,128)(2,1)}, u32[]{:S(2)}, u32[]{:S(2)}) collective-permute-start(bf16[466,8,128]{2,1,0:T(8,128)(2,1)} %get-tuple-element.61), channel_id=1, source_target_pairs={{0,1},{1,0},{2,3},{3,2},{4,5},{5,4},{6,7},{7,6},{8,9},{9,8},{10,11... | collective-permute-start | bytes 2863112 | tf_op jit(solution)/shard_map/ppermute | solution.py:552
  715.1 56.1 %collective-permute-start.65 = (bf16[466,8,128]{2,1,0:T(8,128)(2,1)}, bf16[466,8,128]{2,1,0:T(8,128)(2,1)}, u32[]{:S(2)}, u32[]{:S(2)}) collective-permute-start(bf16[466,8,128]{2,1,0:T(8,128)(2,1)} %get-tuple-element.90), channel_id=1, source_target_pairs={{0,8},{1,9},{2,10},{3,11},{4,12},{5,13},{6,14},{7,15},{8,0},{9,1},... | collective-permute-start | bytes 2863112 | tf_op jit(solution)/shard_map/ppermute | solution.py:552
  729.1 173.9 %collective-permute-start.38 = (bf16[466,8,128]{2,1,0:T(8,128)(2,1)}, bf16[466,8,128]{2,1,0:T(8,128)(2,1)}, u32[]{:S(2)}, u32[]{:S(2)}) collective-permute-start(bf16[466,8,128]{2,1,0:T(8,128)(2,1)} %get-tuple-element.77), channel_id=1, source_target_pairs={{0,16},{1,3},{2,18},{3,1},{4,20},{5,7},{6,22},{7,5},{8,24},{9,11},... | collective-permute-start | bytes 2863112 | tf_op jit(solution)/shard_map/ppermute | solution.py:552
  735.5 167.5 %collective-permute-start.42 = (bf16[466,8,128]{2,1,0:T(8,128)(2,1)}, bf16[466,8,128]{2,1,0:T(8,128)(2,1)}, u32[]{:S(2)}, u32[]{:S(2)}) collective-permute-start(bf16[466,8,128]{2,1,0:T(8,128)(2,1)} %get-tuple-element.85), channel_id=1, source_target_pairs={{0,2},{1,17},{2,0},{3,19},{4,6},{5,21},{6,4},{7,23},{8,10},{9,25},... | collective-permute-start | bytes 2863112 | tf_op jit(solution)/shard_map/ppermute | solution.py:552
  736.4 166.6 %collective-permute-start.50 = (bf16[466,8,128]{2,1,0:T(8,128)(2,1)}, bf16[466,8,128]{2,1,0:T(8,128)(2,1)}, u32[]{:S(2)}, u32[]{:S(2)}) collective-permute-start(bf16[466,8,128]{2,1,0:T(8,128)(2,1)} %get-tuple-element.89), channel_id=1, source_target_pairs={{0,8},{1,9},{2,10},{3,11},{4,12},{5,13},{6,14},{7,15},{8,0},{9,1},... | collective-permute-start | bytes 2863112 | tf_op jit(solution)/shard_map/ppermute | solution.py:552
  775.2 127.8 %collective-permute-start.66 = (bf16[466,8,128]{2,1,0:T(8,128)(2,1)}, bf16[466,8,128]{2,1,0:T(8,128)(2,1)}, u32[]{:S(2)}, u32[]{:S(2)}) collective-permute-start(bf16[466,8,128]{2,1,0:T(8,128)(2,1)} %add_convert_fusion.2), channel_id=1, source_target_pairs={{0,4},{1,5},{2,6},{3,7},{4,0},{5,1},{6,2},{7,3},{8,12},{9,13},{10,... | collective-permute-start | bytes 2863112 | tf_op jit(solution)/shard_map/ppermute | solution.py:552
  (112 other events, 2567.5 us)
Sparse Core Ops, SparseCore 0:
  728.5 171.4 all-reduce.5
